TPU v7x, 512 devices: a whole 4x8x8 slice. The times are simulated.
512 devices in a mesh: sub: 16 (over z_lo, x), row: 32 (over y, z_hi, core).
Axes of the slice: x: 4, y: 8, z: 8 (z_hi: 2, z_lo: 4; z = z_hi * 4 + z_lo), core: 2. Of those that a mesh axis runs over, the one named last changes fastest.
Arguments:
- phi_rows: bfloat16 [524288, 400], P(('sub', 'row')), may hold values from -0.125 to 0.125
- psi_rows: bfloat16 [524288, 1536], P(('sub', 'row')), may hold values from -0.125 to 0.125
- stiffness: bfloat16 [4096, 128, 128], P(('sub', 'row')), may hold values from -0.046875 to 0.046875
- coord_fixed: bfloat16 [16, 256, 400], P('sub', 'row'), may hold values from -6 to 6
- coord_con: bfloat16 [16, 256, 1536], P('sub', 'row'), may hold values from -6 to 6
- elem_zone: int32 [4096], P(('sub', 'row')), may hold values from 0 to 1023
- partner: int32 [4096], P(('sub', 'row')), may hold values from 0 to 7, as said below
- owner_slot: int32 [1024], replicated, may hold values from 0 to 1023, each once
Outputs:
- zone_sens: float32 [1024, 256], P(('sub', 'row'))
Inputs may be any that keep to these rules, and one draw needn't show every extreme that they name: partner[b] differs from b % 8.
All inputs are finite; a program needn't handle non-finite values.
Results may differ from a plain program's by a relative error of at most 0.015.
Values may be sent and summed in bfloat16 or wider, within the bound.
No kernel may reach another device: no remote copies, remote signals or barrier semaphores. Data moves between devices by JAX's collectives and lax.ppermute only.
A program may use at most 64 MiB of HBM per device.

v0:
```python
import jax
import jax.numpy as jnp
from jax import lax
from jax.sharding import PartitionSpec as P


def on_device(
    phi_rows, psi_rows, stiffness, coord_fixed, coord_con, elem_zone, partner, owner_slot
):
    dims = (((1,), (1,)), ((), ()))
    fixed_part, con_part = lax.all_gather((coord_fixed, coord_con), "row", axis=1, tiled=True)
    total = lax.dot_general(phi_rows, fixed_part[0], dims, preferred_element_type=jnp.float32)
    total = total + lax.dot_general(psi_rows, con_part[0], dims, preferred_element_type=jnp.float32)
    shapes = total.astype(jnp.bfloat16)
    nblocks = stiffness.shape[0]
    modes = shapes.shape[1]
    blocks = shapes.reshape(nblocks, stiffness.shape[1], modes)
    other = jnp.take(blocks, partner, axis=0)
    relative = (blocks.astype(jnp.float32) - other.astype(jnp.float32)).astype(jnp.bfloat16)
    pushed = jnp.einsum("bij,bjm->bim", stiffness, relative, preferred_element_type=jnp.float32)
    energy = jnp.sum(relative.astype(jnp.float32) * pushed, axis=1)
    zones = owner_slot.shape[0]
    hits = elem_zone[:, None] == jnp.arange(zones, dtype=jnp.int32)[None, :]
    slots = jnp.sum(jnp.where(hits, owner_slot[None, :], 0), axis=1)
    partial_sums = jnp.zeros((zones, modes), jnp.float32).at[slots].add(energy)
    result = lax.psum_scatter(partial_sums, ("sub", "row"), scatter_dimension=0, tiled=True)
    return result


def solution(mesh):
    placed = (
        P(("sub", "row"), None),
        P(("sub", "row"), None),
        P(("sub", "row"), None, None),
        P("sub", "row", None),
        P("sub", "row", None),
        P(("sub", "row")),
        P(("sub", "row")),
        P(),
    )
    return jax.shard_map(
        on_device, mesh=mesh, in_specs=placed, out_specs=P(("sub", "row"), None), check_vma=False
    )
```

profile of v0, /device:TPU:1, one launch (start us, length us, event | category | flops | bytes accessed | tf_op | source)
XLA Modules:
  0.0 407.8 jit_solution(200131966141404425)
XLA Ops:
  6.5 0.0 copy-start
  6.5 0.0 all-reduce.3.cloned.1.call-start
  6.5 0.8 compare_select_fusion
  7.3 0.8 compare_and_fusion
  8.2 63.9 %all_gather.7 = bf16[1,256,1536]{2,1,0:T(8,128)(2,1)S(1)} all-gather(bf16[1,8,1536]{2,1,0:T(8,128)(2,1)} %param.12), channel_id=1, replica_groups=mesh['sub'=16,'row'=32] {'row'}, dimensions={1}, use_global_device_ids=true | all-gather | bytes 811008 | tf_op jit(solution)/shard_map/all_gather | solution.py:11
  72.1 47.7 %all_gather.6 = bf16[1,256,400]{2,1,0:T(8,128)(2,1)S(1)} all-gather(bf16[1,8,400]{2,1,0:T(8,128)(2,1)} %param.11), channel_id=1, replica_groups=mesh['sub'=16,'row'=32] {'row'}, dimensions={1}, use_global_device_ids=true | all-gather | bytes 211200 | tf_op jit(solution)/shard_map/all_gather | solution.py:11
  119.8 0.9 select_reduce_fusion
  120.7 0.0 copy-done
  120.7 0.0 copy-start.1
  120.7 1.0 fusion.3
  121.7 0.1 copy-done.1
  121.8 0.0 copy-start.2
  121.8 1.3 fusion.1
  123.1 2.4 gather_fusion
  125.5 0.0 copy-done.2
  125.5 2.0 fusion.2
  127.6 1.7 scatter_custom_fusion
  129.2 0.0 all-reduce.3.cloned.1.call-update
  129.3 270.4 %all-reduce.3.cloned.1.call-done = f32[1024,256]{1,0:T(8,128)} async-done(((f32[1024,256]{1,0:T(8,128)}), f32[1024,256]{1,0:T(8,128)}) %all-reduce.3.cloned.1.call-update) | async-done | bytes 1048592
  399.7 1.3 constant_dynamic-slice_fusion
  (2 shorter events, 0.0 us)
Async XLA Ops:
  6.5 114.1 %copy-start = (bf16[1024,1536]{1,0:T(8,128)(2,1)S(1)}, bf16[1024,1536]{1,0:T(8,128)(2,1)}, u32[]{:S(2)}) copy-start(bf16[1024,1536]{1,0:T(8,128)(2,1)} %param.9) | copy-start | bytes 9437188
  6.5 393.1 %all-reduce.3.cloned.1.call-start = ((), (), s32[]{:S(2)}) async-start(), calls=%async_computation | async-start | bytes 2097152
  120.7 1.1 copy-start.1
  121.8 3.7 copy-start.2
Sparse Core Ops, SparseCore 0:
  129.4 270.2 all-reduce.2
where the time goes:
time: 408 us
  waiting for transfers between devices  270 us (66%)
  blocking collectives  112 us (27%)
  between operations  13.4 us (3%)
  matrix products  4.3 us (1%)
  other arithmetic  4.19 us (1%)
    unnamed x2, waiting for transfers between devices  270 us
    all_gather x2, blocking collectives, on_device(): lax.all_gather((coord_fixed, coord_con), 'row', axis=1, tiled=True)  112 us
  transfers between devices with their start and end apart: 1, of which 1 were waited for; matrix products, arithmetic and copies ran while one was open for 0% of the time, Pallas kernels for 0%

commit v1 on v0

v1 whole, which is shorter than its diff:
```python
import jax
import jax.numpy as jnp
from jax import lax
from jax.experimental import pallas as pl
from jax.experimental.pallas import tpu as pltpu
from jax.sharding import Mesh, PartitionSpec as P

AXES = ("zlo", "x", "y", "zhi", "core")
SIZES = (4, 4, 8, 2, 2)
ROW = ("y", "zhi", "core")
REST = ("zlo", "x", "zhi", "core")
NT = (((1,), (1,)), ((), ()))


def energy_kernel(partner_ref, shapes_ref, stiffness_ref, out_ref):
    nblocks = shapes_ref.shape[0]
    rows = []
    for b in range(nblocks):
        own = shapes_ref[b].astype(jnp.float32)
        other = shapes_ref[partner_ref[b]].astype(jnp.float32)
        relative = (own - other).astype(jnp.bfloat16)
        pushed = jnp.dot(stiffness_ref[b], relative, preferred_element_type=jnp.float32)
        rows.append(jnp.sum(relative.astype(jnp.float32) * pushed, axis=0, keepdims=True))
    energy = jnp.concatenate(rows, axis=0).astype(jnp.bfloat16)
    for i in range(out_ref.shape[0]):
        out_ref[i] = energy


def block_energy(partner, shapes, stiffness, copies):
    nblocks, _, modes = shapes.shape
    vmem = pl.BlockSpec(memory_space=pltpu.VMEM)
    return pl.pallas_call(
        energy_kernel,
        out_shape=jax.ShapeDtypeStruct((copies, nblocks, modes), jnp.bfloat16),
        in_specs=[pl.BlockSpec(memory_space=pltpu.SMEM), vmem, vmem],
        out_specs=vmem,
        compiler_params=pltpu.CompilerParams(vmem_limit_bytes=16 * 2**20),
        cost_estimate=pl.CostEstimate(flops=2 * nblocks * 128 * 128 * modes, bytes_accessed=2**20, transcendentals=0),
    )(partner, shapes, stiffness)


def on_device(
    phi_rows, psi_rows, stiffness, coord_fixed, coord_con, elem_zone, partner, owner_slot
):
    nblocks, block, _ = stiffness.shape
    nf, nc = coord_fixed.shape[2], coord_con.shape[2]
    mine = coord_fixed.shape[1]
    zones = owner_slot.shape[0]
    n_row = 32
    modes = n_row * mine

    hits = elem_zone[:, None] == jnp.arange(zones, dtype=jnp.int32)[None, :]
    slots = jnp.sum(jnp.where(hits, owner_slot[None, :], 0), axis=1)
    coded = jnp.stack([slots // 32, slots % 32], axis=1).astype(jnp.bfloat16)
    pad = -(nc + nf + 2) % 128
    packet = jnp.concatenate(
        [coord_con[0], coord_fixed[0], coded, jnp.zeros((mine, pad), jnp.bfloat16)], axis=1
    )
    gathered = lax.all_to_all(
        jnp.broadcast_to(packet[None], (n_row, *packet.shape)), ROW, 0, 0, tiled=True
    )
    coords = gathered.reshape(modes, -1)

    total = lax.dot_general(psi_rows, coords[:, :nc], NT, preferred_element_type=jnp.float32)
    total = total + lax.dot_general(
        phi_rows, coords[:, nc : nc + nf], NT, preferred_element_type=jnp.float32
    )
    shapes = total.astype(jnp.bfloat16).reshape(nblocks, block, modes)
    n_y = 8
    energy = block_energy(partner, shapes, stiffness, n_y)

    along_y = lax.all_to_all(energy, "y", 0, 0, tiled=True).reshape(n_y * nblocks, modes)
    kept = gathered[:, :, nc + nf : nc + nf + 2].reshape(n_y, 4, nblocks, 2).astype(jnp.int32)
    at = lax.axis_index("zhi") * 2 + lax.axis_index("core")
    kept = lax.dynamic_index_in_dim(kept, at, axis=1, keepdims=False)
    block_slots = (kept[:, :, 0] * 32 + kept[:, :, 1]).reshape(n_y * nblocks)
    n_rest = 64
    dest = jnp.arange(2 * n_rest, dtype=jnp.int32)
    peer = dest // 2
    owned = 2 * ((peer // 4) * n_row + lax.axis_index("y") * 4 + peer % 4) + dest % 2
    chosen = (owned[:, None] == block_slots[None, :]).astype(jnp.bfloat16)
    partial_sums = jnp.dot(chosen, along_y, preferred_element_type=jnp.float32)
    partial_sums = partial_sums.astype(jnp.bfloat16).reshape(n_rest, 2, modes)
    received = lax.all_to_all(partial_sums, REST, 0, 0, tiled=True)
    return jnp.sum(received.astype(jnp.float32), axis=0)


def solution(mesh):
    fine = Mesh(mesh.devices.reshape(SIZES), AXES)
    sub, row = AXES[:2], AXES[2:]
    placed = (
        P(AXES, None),
        P(AXES, None),
        P(AXES, None, None),
        P(sub, row, None),
        P(sub, row, None),
        P(AXES),
        P(AXES),
        P(),
    )
    return jax.shard_map(
        on_device, mesh=fine, in_specs=placed, out_specs=P(AXES, None), check_vma=False
    )
```

time: 408 us -> 91.8 us (0.23)
  waiting for transfers between devices: 270 us -> 36.1 us
  blocking collectives: 112 us -> 18.8 us
  starting transfers between devices: 0.01 us -> 21.9 us
  between operations: 13.4 us -> 0.09 us
    unnamed x2 -> x0, waiting for transfers between devices: 270 us -> none
    all_gather x2 -> x0, blocking collectives: 112 us -> none  [on_device(): lax.all_gather((coord_fixed, coord_con), 'row', axis=1, tiled=True)]
    all_to_all x0 -> x2, waiting for transfers between devices: none -> 36.1 us  [the longest x1 30.6 us: on_device(): lax.all_to_all(jnp.broadcast_to(packet[None], (n_row, *packet.shape)), RO...]
    all_to_all x0 -> x2, starting transfers between devices: none -> 21.9 us  [the longest x1 17.3 us: on_device(): lax.all_to_all(jnp.broadcast_to(packet[None], (n_row, *packet.shape)), RO...]
    all_to_all x0 -> x1, blocking collectives: none -> 18.8 us  [on_device(): received = lax.all_to_all(partial_sums, REST, 0, 0, tiled=True)]
  transfers between devices with their start and end apart: 1 -> 2, of which waited for: 1 -> 2; matrix products, arithmetic and copies ran while one was open for 0% -> 1% of each run, Pallas kernels for 0% -> 0%
where the time goes in v1:
time: 91.8 us; the launch traced here: 91.4 us
  waiting for transfers between devices  36.1 us (39%)
  starting transfers between devices  21.9 us (24%)
  blocking collectives  18.8 us (20%)
  local copies, waits for them, and re-layouts  6.56 us (7%)
  matrix products  4.65 us (5%)
  other arithmetic  1.76 us (2%)
  Pallas kernels  1.47 us (2%)
    all_to_all x1, waiting for transfers between devices, on_device(): lax.all_to_all(jnp.broadcast_to(packet[None], (n_row, *packet.shape)), RO...  30.6 us
    all_to_all x1, blocking collectives, on_device(): received = lax.all_to_all(partial_sums, REST, 0, 0, tiled=True)  18.8 us
    all_to_all x1, starting transfers between devices, on_device(): lax.all_to_all(jnp.broadcast_to(packet[None], (n_row, *packet.shape)), RO...  17.3 us
    all_to_all x1, waiting for transfers between devices, on_device(): lax.all_to_all(energy, 'y', 0, 0, tiled=True).reshape(n_y * nblocks, modes)  5.54 us
    all_to_all x1, starting transfers between devices, on_device(): lax.all_to_all(energy, 'y', 0, 0, tiled=True).reshape(n_y * nblocks, modes)  4.65 us
    dot_general x1, matrix products, on_device(): lax.dot_general(phi_rows, coords[:, nc:nc + nf], NT, preferred_element_ty...  2.24 us
    dot_general x1, matrix products, on_device(): lax.dot_general(psi_rows, coords[:, :nc], NT, preferred_element_type=jnp....  2.21 us
    convert_element_type x1, local copies, waits for them, and re-layouts, on_device(): shapes = total.astype(jnp.bfloat16).reshape(nblocks, block, modes)  2.03 us
  transfers between devices with their start and end apart: 2, of which 2 were waited for; matrix products, arithmetic and copies ran while one was open for 1% of the time, Pallas kernels for 0%

profile of v1, /device:TPU:1, one launch (start us, length us, event | category | flops | bytes accessed | tf_op | source)
XLA Modules:
  0.0 91.4 jit_solution(13578315960170310221)
XLA Ops:
  0.0 0.0 copy-start
  0.0 1.0 %select_reduce_fusion = s32[8]{0:T(128)S(1)} fusion(s32[1024]{0:T(1024)} %param.15, s32[8]{0:T(128)} %param.13), kind=kLoop, calls=%fused_computation.11 | loop fusion | flops 24568 | bytes 4160 | tf_op jit(solution)/shard_map/reduce_sum | solution.py:53
  1.0 0.1 copy.25
  1.1 0.1 copy.26
  1.2 0.8 concatenate.4
  2.1 1.1 %broadcast_in_dim.28 = bf16[32,8,2048]{2,1,0:T(8,128)(2,1)} broadcast(bf16[8,2048]{1,0:T(8,128)(2,1)S(1)} %concatenate.4), dimensions={1,2} | broadcast | bytes 1081344 | tf_op jit(solution)/shard_map/broadcast_in_dim | solution.py:60
  3.2 17.3 %all-to-all-start = ((bf16[32,8,2048]{2,1,0:T(8,128)(2,1)}), bf16[32,8,2048]{2,1,0:T(8,128)(2,1)}, u32[]{:S(2)}, u32[]{:S(2)}) async-start(bf16[32,8,2048]{2,1,0:T(8,128)(2,1)} %broadcast_in_dim.28), calls=%async_computation | async-start | bytes 2097152 | tf_op jit(solution)/shard_map/all_to_all | solution.py:59
  20.5 30.6 %all-to-all-done = bf16[32,8,2048]{2,1,0:T(8,128)(2,1)} async-done(((bf16[32,8,2048]{2,1,0:T(8,128)(2,1)}), bf16[32,8,2048]{2,1,0:T(8,128)(2,1)}, u32[]{:S(2)}, u32[]{:S(2)}) %all-to-all-start) | async-done | bytes 1048608 | tf_op jit(solution)/shard_map/all_to_all | solution.py:59
  51.1 0.0 copy-start.4
  51.1 0.0 copy-done
  51.1 2.2 %fusion.2 = f32[256,1024]{1,0:T(8,128)S(1)} fusion(bf16[1024,1536]{1,0:T(8,128)(2,1)S(1)} %copy-done, bf16[256,2048]{1,0:T(8,128)(2,1)} %bitcast.5), kind=kOutput, calls=%fused_computation.4 | convolution fusion | flops 805306368 | bytes 4980736 | tf_op jit(solution)/shard_map/dot_general | solution.py:64
  53.3 0.0 copy-done.4
  53.3 0.0 copy-start.2
  53.3 0.0 copy-start.3
  53.3 2.2 %fusion.1 = bf16[1024,256]{0,1:T(8,128)(2,1)} fusion(f32[256,1024]{1,0:T(8,128)S(1)} %fusion.2, bf16[1024,400]{0,1:T(8,128)(2,1)S(1)} %copy-done.4, bf16[256,2048]{1,0:T(8,128)(2,1)} %bitcast.5), kind=kOutput, calls=%fused_computation.2 | convolution fusion | flops 210239488 | bytes 2654208 | tf_op jit(solution)/shard_map/dot_general | solution.py:65
  55.6 2.0 %copy.28 = bf16[1024,256]{1,0:T(8,128)(2,1)} copy(bf16[1024,256]{0,1:T(8,128)(2,1)} %fusion.1) | data formatting | bytes 1048576 | tf_op jit(solution)/shard_map/convert_element_type | solution.py:68
  57.6 0.0 copy-done.2
  57.6 0.0 copy-done.3
  57.6 0.0 copy-start.1
  57.6 1.0 %copy-done.1 = bf16[1024,256]{1,0:T(8,128)(2,1)S(1)} copy-done((bf16[1024,256]{1,0:T(8,128)(2,1)S(1)}, bf16[1024,256]{1,0:T(8,128)(2,1)}, u32[]{:S(2)}) %copy-start.1) | copy-done | bytes 524312
  58.6 1.5 %shard_map.82 = bf16[8,8,256]{2,1,0:T(8,128)(2,1)} custom-call(s32[8]{0:T(128)S(1)} %copy-done.3, bf16[8,128,256]{2,1,0:T(8,128)(2,1)S(1)} %bitcast.33, bf16[8,128,128]{2,1,0:T(8,128)(2,1)S(1)} %copy-done.2), custom_call_target="tpu_custom_call" | custom-call | flops 67108864 | bytes 1048576 | tf_op jit(solution)/shard_map/pallas_call | solution.py:32
  60.1 4.7 %all-to-all-start.1 = ((bf16[8,8,256]{2,1,0:T(8,128)(2,1)}), bf16[8,8,256]{2,1,0:T(8,128)(2,1)S(1)}, u32[]{:S(2)}, u32[]{:S(2)}) async-start(bf16[8,8,256]{2,1,0:T(8,128)(2,1)} %shard_map.82), calls=%async_computation.1 | async-start | bytes 65536 | tf_op jit(solution)/shard_map/all_to_all | solution.py:72
  64.8 0.9 %slice.20 = bf16[32,8,2]{2,1,0:T(8,128)(2,1)S(1)} slice(bf16[32,8,2048]{2,1,0:T(8,128)(2,1)} %all-to-all-done), slice={[0:32], [0:8], [1936:1938]} | slice | bytes 2048 | tf_op jit(solution)/shard_map/slice | solution.py:73
  65.7 0.3 copy.29
  66.0 0.1 add.104
  66.1 5.5 %all-to-all-done.1 = bf16[8,8,256]{2,1,0:T(8,128)(2,1)S(1)} async-done(((bf16[8,8,256]{2,1,0:T(8,128)(2,1)}), bf16[8,8,256]{2,1,0:T(8,128)(2,1)S(1)}, u32[]{:S(2)}, u32[]{:S(2)}) %all-to-all-start.1) | async-done | bytes 32800 | tf_op jit(solution)/shard_map/all_to_all | solution.py:72
  71.6 0.2 convolution_convert_fusion
  71.9 18.8 %all_to_all.15 = bf16[64,2,256]{2,1,0:T(2,128)(2,1)S(1)} all-to-all(bf16[64,2,256]{2,1,0:T(2,128)(2,1)S(1)} %reshape.157), channel_id=1, replica_groups=mesh['zlo'=4,'x'=4,'y'=8,'zhi'=2,'core'=2] {'zlo','x','zhi','core'}, dimensions={0} | all-to-all | bytes 131072 | tf_op jit(solution)/shard_map/all_to_all | solution.py:84
  90.7 0.7 convert_reduce_fusion
  (6 shorter events, 0.1 us)
Async XLA Ops:
  0.0 51.1 %copy-start = (bf16[1024,1536]{1,0:T(8,128)(2,1)S(1)}, bf16[1024,1536]{1,0:T(8,128)(2,1)}, u32[]{:S(2)}) copy-start(bf16[1024,1536]{1,0:T(8,128)(2,1)} %param.9) | copy-start | bytes 9437188
  3.2 47.9 %all-to-all-start = ((bf16[32,8,2048]{2,1,0:T(8,128)(2,1)}), bf16[32,8,2048]{2,1,0:T(8,128)(2,1)}, u32[]{:S(2)}, u32[]{:S(2)}) async-start(bf16[32,8,2048]{2,1,0:T(8,128)(2,1)} %broadcast_in_dim.28), calls=%async_computation | async-start | bytes 2097152 | tf_op jit(solution)/shard_map/all_to_all | solution.py:59
  51.1 2.2 %copy-start.4 = (bf16[1024,400]{0,1:T(8,128)(2,1)S(1)}, bf16[1024,400]{0,1:T(8,128)(2,1)}, u32[]{:S(2)}) copy-start(bf16[1024,400]{0,1:T(8,128)(2,1)} %param.8) | copy-start | bytes 2457604
  53.3 4.3 %copy-start.2 = (bf16[8,128,128]{2,1,0:T(8,128)(2,1)S(1)}, bf16[8,128,128]{2,1,0:T(8,128)(2,1)}, u32[]{:S(2)}) copy-start(bf16[8,128,128]{2,1,0:T(8,128)(2,1)} %stiffness_ref.1) | copy-start | bytes 786436
  53.3 4.3 %copy-start.3 = (s32[8]{0:T(128)S(1)}, s32[8]{0:T(128)}, u32[]{:S(2)}) copy-start(s32[8]{0:T(128)} %partner_ref.1) | copy-start | bytes 100
  57.6 1.0 %copy-start.1 = (bf16[1024,256]{1,0:T(8,128)(2,1)S(1)}, bf16[1024,256]{1,0:T(8,128)(2,1)}, u32[]{:S(2)}) copy-start(bf16[1024,256]{1,0:T(8,128)(2,1)} %copy.28) | copy-start | bytes 1572868
  60.1 11.5 %all-to-all-start.1 = ((bf16[8,8,256]{2,1,0:T(8,128)(2,1)}), bf16[8,8,256]{2,1,0:T(8,128)(2,1)S(1)}, u32[]{:S(2)}, u32[]{:S(2)}) async-start(bf16[8,8,256]{2,1,0:T(8,128)(2,1)} %shard_map.82), calls=%async_computation.1 | async-start | bytes 65536 | tf_op jit(solution)/shard_map/all_to_all | solution.py:72

commit v2 on v0

v2 whole, which is shorter than its diff:
```python
import jax
import jax.numpy as jnp
from jax import lax
from jax.experimental import pallas as pl
from jax.experimental.pallas import tpu as pltpu
from jax.sharding import Mesh, PartitionSpec as P

AXES = ("zlo", "x", "y", "zhi", "core")
SIZES = (4, 4, 8, 2, 2)
N_ROW = 32
NT = (((1,), (1,)), ((), ()))
TN = (((0,), (0,)), ((), ()))
VMEM = pl.BlockSpec(memory_space=pltpu.VMEM)
SMEM = pl.BlockSpec(memory_space=pltpu.SMEM)
CODE_LANES = 128


def packet_kernel(con_ref, fixed_ref, out_ref):
    mine, nf = fixed_ref.shape
    nc = con_ref.shape[1]
    whole = nf // 128 * 128
    head = jnp.concatenate([con_ref[...], fixed_ref[:, :whole]], axis=1)
    blank = jnp.zeros((mine, out_ref.shape[2] - nc - nf), out_ref.dtype)
    tail = jnp.concatenate([fixed_ref[:, whole:], blank], axis=1)
    for i in range(out_ref.shape[0]):
        out_ref[i, :, : nc + whole] = head
        out_ref[i, :, nc + whole :] = tail


def packets(con, fixed, copies, width):
    return pl.pallas_call(
        packet_kernel,
        out_shape=jax.ShapeDtypeStruct((copies, con.shape[0], width), con.dtype),
        in_specs=[VMEM, VMEM],
        out_specs=VMEM,
        compiler_params=pltpu.CompilerParams(vmem_limit_bytes=56 * 2**20),
    )(con, fixed)


def early_kernel(elem_zone_ref, owner_slot_ref, phi_ref, rows_ref, codes_ref):
    nf, rows = phi_ref.shape
    rows_ref[:, :nf] = phi_ref[...].T
    rows_ref[:, nf:] = jnp.zeros((rows, rows_ref.shape[1] - nf), rows_ref.dtype)
    row = lax.broadcasted_iota(jnp.int32, codes_ref.shape, 0)
    lane = lax.broadcasted_iota(jnp.int32, codes_ref.shape, 1)
    codes = jnp.zeros(codes_ref.shape, jnp.int32)
    for b in range(codes_ref.shape[0]):
        slot = owner_slot_ref[elem_zone_ref[b]]
        codes = jnp.where((row == b) & (lane == 0), slot // 32, codes)
        codes = jnp.where((row == b) & (lane == 1), slot % 32, codes)
    codes_ref[...] = codes.astype(jnp.float32).astype(codes_ref.dtype)


def early(elem_zone, owner_slot, phi_t, width):
    return pl.pallas_call(
        early_kernel,
        out_shape=(
            jax.ShapeDtypeStruct((phi_t.shape[1], width), phi_t.dtype),
            jax.ShapeDtypeStruct((elem_zone.shape[0], CODE_LANES), jnp.bfloat16),
        ),
        in_specs=[SMEM, SMEM, VMEM],
        out_specs=(VMEM, VMEM),
        compiler_params=pltpu.CompilerParams(vmem_limit_bytes=16 * 2**20),
        cost_estimate=pl.CostEstimate(flops=0, bytes_accessed=8 * 2**20, transcendentals=0),
    )(elem_zone, owner_slot, phi_t)


def own_shapes_kernel(own_ref, phi_ref, psi_ref, shapes_ref, kept_ref, arrived):
    rows, nc = psi_ref.shape
    chunks = arrived.shape[0]
    step = rows // chunks
    parts = [pl.ds(i * step, step) for i in range(chunks)]
    copies = [
        pltpu.make_async_copy(psi_ref.at[part], kept_ref.at[part], arrived.at[i])
        for i, part in enumerate(parts)
    ]
    for copy in copies:
        copy.start()
    for part, copy in zip(parts, copies):
        total = lax.dot_general(
            phi_ref[part], own_ref[:, nc:], NT, preferred_element_type=jnp.float32
        )
        copy.wait()
        total = total + lax.dot_general(
            kept_ref[part], own_ref[:, :nc], NT, preferred_element_type=jnp.float32
        )
        shapes_ref[part] = total.astype(shapes_ref.dtype)


def own_shapes(own, phi, psi, chunks=4):
    rows, nc = psi.shape
    return pl.pallas_call(
        own_shapes_kernel,
        out_shape=(
            pltpu.VMEM((rows, own.shape[0]), jnp.bfloat16),
            pltpu.VMEM((rows, nc), psi.dtype),
        ),
        in_specs=[VMEM, VMEM, pl.BlockSpec(memory_space=pltpu.HBM)],
        out_specs=(VMEM, VMEM),
        scratch_shapes=[pltpu.SemaphoreType.DMA((chunks,))],
        compiler_params=pltpu.CompilerParams(vmem_limit_bytes=52 * 2**20),
        cost_estimate=pl.CostEstimate(flops=2**29, bytes_accessed=5 * 2**20, transcendentals=0),
    )(own, phi, psi)


def energy_kernel(
    partner_ref, other_ref, phi_ref, psi_ref, own_shapes_ref, stiffness_ref, codes_ref, out_ref, shapes
):
    half = other_ref.shape[0]
    nc = psi_ref.shape[1]
    nblocks, block, _ = stiffness_ref.shape
    modes = 2 * half
    total = lax.dot_general(phi_ref[...], other_ref[:, nc:], NT, preferred_element_type=jnp.float32)
    total = total + lax.dot_general(
        psi_ref[...], other_ref[:, :nc], NT, preferred_element_type=jnp.float32
    )
    for b in range(nblocks):
        part = slice(b * block, (b + 1) * block)
        shapes[b, :, :half] = own_shapes_ref[part]
        shapes[b, :, half:] = total[part].astype(shapes.dtype)
    sums = []
    for b in range(nblocks):
        own = shapes[b].astype(jnp.float32)
        partner = shapes[partner_ref[b]].astype(jnp.float32)
        relative = (own - partner).astype(jnp.bfloat16)
        pushed = jnp.dot(stiffness_ref[b], relative, preferred_element_type=jnp.float32)
        sums.append(jnp.sum(relative.astype(jnp.float32) * pushed, axis=0, keepdims=True))
    energy = jnp.concatenate(sums, axis=0).astype(jnp.bfloat16)
    source = lax.broadcasted_iota(jnp.int32, (modes, modes), 0)
    target = lax.broadcasted_iota(jnp.int32, (modes, modes), 1)
    core = (source // half + lax.axis_index("core")) % 2
    ordered = (source % half) // 8 * 16 + core * 8 + source % 8
    move = (ordered == target).astype(jnp.float32).astype(jnp.bfloat16)
    energy = jnp.dot(energy, move, preferred_element_type=jnp.float32).astype(jnp.bfloat16)
    for i in range(out_ref.shape[0]):
        out_ref[i, :, :modes] = energy
        out_ref[i, :, modes:] = codes_ref[...]


def block_energy(partner, other, phi, psi, shapes, stiffness, codes, copies):
    nblocks, block, _ = stiffness.shape
    modes = 2 * other.shape[0]
    return pl.pallas_call(
        energy_kernel,
        out_shape=jax.ShapeDtypeStruct((copies, nblocks, modes + CODE_LANES), jnp.bfloat16),
        in_specs=[SMEM, VMEM, VMEM, VMEM, VMEM, VMEM, VMEM],
        out_specs=VMEM,
        scratch_shapes=[pltpu.VMEM((nblocks, block, modes), jnp.bfloat16)],
        compiler_params=pltpu.CompilerParams(vmem_limit_bytes=24 * 2**20),
        cost_estimate=pl.CostEstimate(flops=2**30, bytes_accessed=6 * 2**20, transcendentals=0),
    )(partner, other, phi, psi, shapes, stiffness, codes)


def zone_kernel(packet_ref, out_ref):
    peers, nblocks, width = packet_ref.shape
    modes = width - CODE_LANES
    packet = packet_ref[...].astype(jnp.float32).reshape(peers * nblocks, width)
    slot = packet[:, modes : modes + 1] * 32.0 + packet[:, modes + 1 : modes + 2]
    place = lax.broadcasted_iota(jnp.int32, (1, out_ref.shape[0]), 1)
    corner = lax.axis_index("zlo") * 256 + lax.axis_index("zhi") * 4 + lax.axis_index("core") * 2
    owned = (corner + place // 2 * 8 + place % 2).astype(jnp.float32)
    chosen = (slot == owned).astype(jnp.float32).astype(jnp.bfloat16)
    energy = packet[:, :modes].astype(jnp.bfloat16)
    sums = lax.dot_general(chosen, energy, TN, preferred_element_type=jnp.float32)
    out_ref[...] = sums.astype(out_ref.dtype)


def zone_sums(packet, slots):
    return pl.pallas_call(
        zone_kernel,
        out_shape=jax.ShapeDtypeStruct((slots, packet.shape[2] - CODE_LANES), jnp.bfloat16),
        in_specs=[VMEM],
        out_specs=VMEM,
        compiler_params=pltpu.CompilerParams(vmem_limit_bytes=8 * 2**20),
    )(packet)


def on_device(
    phi_rows, psi_rows, stiffness, coord_fixed, coord_con, elem_zone, partner, owner_slot
):
    nf, nc = coord_fixed.shape[2], coord_con.shape[2]
    mine = coord_fixed.shape[1]
    modes = N_ROW * mine
    width = nc + nf + -(nc + nf) % 128

    sent = packets(coord_con[0], coord_fixed[0], N_ROW // 2, width)
    own = lax.all_to_all(sent, ("y", "zhi"), 0, 0, tiled=True).reshape(modes // 2, width)

    phi, codes = early(elem_zone, owner_slot, phi_rows.T, width - nc)
    own, phi, codes = lax.optimization_barrier((own, phi, codes))
    other = lax.ppermute(own, "core", [(0, 1), (1, 0)])

    shapes, psi = own_shapes(own, phi, psi_rows)
    energy = block_energy(partner, other, phi, psi, shapes, stiffness, codes, 16)
    along_z = lax.all_to_all(energy, ("zlo", "zhi", "core"), 0, 0, tiled=True)
    partial_sums = zone_sums(along_z, 64).reshape(32, 2, modes)
    received = lax.all_to_all(partial_sums, ("x", "y"), 0, 0, tiled=True)
    return jnp.sum(received.astype(jnp.float32), axis=0)


def solution(mesh):
    fine = Mesh(mesh.devices.reshape(SIZES), AXES)
    sub, row = AXES[:2], AXES[2:]
    placed = (
        P(AXES, None),
        P(AXES, None),
        P(AXES, None, None),
        P(sub, row, None),
        P(sub, row, None),
        P(AXES),
        P(AXES),
        P(),
    )
    return jax.shard_map(
        on_device, mesh=fine, in_specs=placed, out_specs=P(AXES, None), check_vma=False
    )
```

time: 408 us -> 80.5 us (0.20)
  waiting for transfers between devices: 270 us -> 16.6 us
  blocking collectives: 112 us -> 28.6 us
  starting transfers between devices: 0.01 us -> 19.8 us
  between operations: 13.4 us -> 0.1 us
  Pallas kernels: 0 us -> 10.8 us
  matrix products: 4.3 us -> 0 us
    unnamed x2 -> x0, waiting for transfers between devices: 270 us -> none
    all_gather x2 -> x0, blocking collectives: 112 us -> none  [on_device(): lax.all_gather((coord_fixed, coord_con), 'row', axis=1, tiled=True)]
    all_to_all x0 -> x2, blocking collectives: none -> 28.6 us  [the longest x1 16.2 us: on_device(): received = lax.all_to_all(partial_sums, ('x', 'y'), 0, 0, tiled=True)]
    all_to_all x0 -> x1, waiting for transfers between devices: none -> 16.6 us  [on_device(): lax.all_to_all(sent, ('y', 'zhi'), 0, 0, tiled=True)]
    all_to_all x0 -> x1, starting transfers between devices: none -> 16.3 us  [on_device(): lax.all_to_all(sent, ('y', 'zhi'), 0, 0, tiled=True)]
    pallas_call x0 -> x5, Pallas kernels: none -> 10.8 us  [the longest x1 5.39 us: own_shapes(): pl.pallas_call(own_shapes_kernel, out_shape=(pltpu.VMEM((rows, own.shape[...]
    dot_general x3 -> x0, matrix products: 4.3 us -> none  [the longest x1 2 us: on_device(): jnp.einsum('bij,bjm->bim', stiffness, relative, preferred_element_type=jn...]
  transfers between devices with their start and end apart: 1 -> 2, of which waited for: 1 -> 1; matrix products, arithmetic and copies ran while one was open for 0% -> 0% of each run, Pallas kernels for 0% -> 8%
where the time goes in v2:
time: 80.5 us; the launch traced here: 80 us
  blocking collectives  28.6 us (36%)
  starting transfers between devices  19.8 us (25%)
  waiting for transfers between devices  16.6 us (21%)
  Pallas kernels  10.8 us (13%)
  local copies, waits for them, and re-layouts  3.49 us (4%)
    all_to_all x1, waiting for transfers between devices, on_device(): lax.all_to_all(sent, ('y', 'zhi'), 0, 0, tiled=True)  16.6 us
    all_to_all x1, starting transfers between devices, on_device(): lax.all_to_all(sent, ('y', 'zhi'), 0, 0, tiled=True)  16.3 us
    all_to_all x1, blocking collectives, on_device(): received = lax.all_to_all(partial_sums, ('x', 'y'), 0, 0, tiled=True)  16.2 us
    all_to_all x1, blocking collectives, on_device(): along_z = lax.all_to_all(energy, ('zlo', 'zhi', 'core'), 0, 0, tiled=True)  12.4 us
    pallas_call x1, Pallas kernels, own_shapes(): pl.pallas_call(own_shapes_kernel, out_shape=(pltpu.VMEM((rows, own.shape[...  5.39 us
    unnamed x16, local copies, waits for them, and re-layouts  3.46 us
    ppermute x1, starting transfers between devices, on_device(): other = lax.ppermute(own, 'core', [(0, 1), (1, 0)])  3.45 us
    pallas_call x1, Pallas kernels, block_energy(): pl.pallas_call(energy_kernel, out_shape=jax.ShapeDtypeStruct((copies, nbl...  2.51 us
  transfers between devices with their start and end apart: 2, of which 1 were waited for; matrix products, arithmetic and copies ran while one was open for 0% of the time, Pallas kernels for 8%

profile of v2, /device:TPU:1, one launch (start us, length us, event | category | flops | bytes accessed | tf_op | source)
XLA Modules:
  0.0 80.0 jit_solution(15698959958622889012)
XLA Ops:
  0.0 1.6 %shard_map.82 = bf16[16,8,2048]{2,1,0:T(8,128)(2,1)} custom-call(bf16[8,1536]{1,0:T(8,128)(2,1)} %bitcast.7, bf16[8,400]{1,0:T(8,128)(2,1)} %bitcast.8), custom_call_target="tpu_custom_call" | custom-call | tf_op jit(solution)/shard_map/pallas_call | solution.py:31
  1.6 0.0 copy-start.3
  1.6 0.0 copy-start.5
  1.6 16.3 %all-to-all-start = ((bf16[16,8,2048]{2,1,0:T(8,128)(2,1)}), bf16[16,8,2048]{2,1,0:T(8,128)(2,1)S(1)}, u32[]{:S(2)}, u32[]{:S(2)}) async-start(bf16[16,8,2048]{2,1,0:T(8,128)(2,1)} %shard_map.82), calls=%async_computation | async-start | bytes 1048576 | tf_op jit(solution)/shard_map/all_to_all | solution.py:187
  18.0 0.0 copy-start.2
  18.0 1.1 %copy-done.2 = bf16[1024,400]{0,1:T(8,128)(2,1)S(1)} copy-done((bf16[1024,400]{0,1:T(8,128)(2,1)S(1)}, bf16[1024,400]{0,1:T(8,128)(2,1)}, u32[]{:S(2)}) %copy-start.2) | copy-done | bytes 819224
  19.1 0.0 copy-start.4
  19.1 0.7 copy-done.4
  19.8 0.0 copy-start.6
  19.8 0.7 copy-done.6
  20.5 0.9 %shard_map.83 = (bf16[1024,512]{1,0:T(8,128)(2,1)S(1)}, bf16[8,128]{1,0:T(8,128)(2,1)S(1)}) custom-call(s32[8]{0:T(128)S(1)} %copy-done.6, s32[1024]{0:T(1024)S(1)} %copy-done.4, bf16[400,1024]{1,0:T(8,128)(2,1)S(1)} %bitcast.4), custom_call_target="tpu_custom_call" | custom-call | bytes 8388608 | tf_op jit(solution)/shard_map/pallas_call | solution.py:55
  21.4 0.0 copy-start
  21.4 1.0 %copy-done = bf16[1024,512]{1,0:T(8,128)(2,1)} copy-done((bf16[1024,512]{1,0:T(8,128)(2,1)}, bf16[1024,512]{1,0:T(8,128)(2,1)S(1)}, u32[]{:S(2)}) %copy-start) | copy-done | bytes 1048600
  22.4 16.6 %all-to-all-done = bf16[16,8,2048]{2,1,0:T(8,128)(2,1)S(1)} async-done(((bf16[16,8,2048]{2,1,0:T(8,128)(2,1)}), bf16[16,8,2048]{2,1,0:T(8,128)(2,1)S(1)}, u32[]{:S(2)}, u32[]{:S(2)}) %all-to-all-start) | async-done | bytes 524320 | tf_op jit(solution)/shard_map/all_to_all | solution.py:187
  39.0 0.0 copy-start.7
  39.0 0.0 copy-start.1
  39.0 3.4 %collective-permute-start = (bf16[128,2048]{1,0:T(8,128)(2,1)S(1)}, bf16[128,2048]{1,0:T(8,128)(2,1)S(1)}, u32[]{:S(2)}, u32[]{:S(2)}) collective-permute-start(bf16[128,2048]{1,0:T(8,128)(2,1)S(1)} %bitcast.5), channel_id=1, source_target_pairs={{0,1},{1,0},{2,3},{3,2},{4,5},{5,4},{6,7},{7,6},{8,9},{9,8},{10,11... | collective-permute-start | bytes 1572872 | tf_op jit(solution)/shard_map/ppermute | solution.py:191
  42.4 0.0 copy-done.7
  42.4 5.4 %shard_map.84 = (bf16[1024,128]{1,0:T(8,128)(2,1)S(1)}, bf16[1024,1536]{1,0:T(8,128)(2,1)S(1)}) custom-call(bf16[128,2048]{1,0:T(8,128)(2,1)} %bitcast.6, bf16[1024,512]{1,0:T(8,128)(2,1)} %copy-done, bf16[1024,1536]{1,0:T(8,128)(2,1)} %psi_ref.1), custom_call_target="tpu_custom_call" | custom-call | flops 536870912 | bytes 5242880 | tf_op jit(solution)/shard_map/pallas_call | solution.py:92
  47.8 0.0 collective-permute-done.other_ref
  47.8 0.0 copy-done.3
  47.9 0.0 copy-done.5
  47.9 0.0 copy-done.1
  47.9 2.5 %shard_map.85 = bf16[16,8,384]{2,1,0:T(8,128)(2,1)S(1)} custom-call(s32[8]{0:T(128)S(1)} %copy-done.5, bf16[128,2048]{1,0:T(8,128)(2,1)S(1)} %collective-permute-done.other_ref, bf16[1024,512]{1,0:T(8,128)(2,1)S(1)} %copy-done.1, bf16[1024,1536]{1,0:T(8,128)(2,1)S(1)} %get-tuple-element.16.psi_ref, bf16[1024,128]{1,0:T(8,128)(2,1)S(1)} %get-tuple-element.17.own_shapes_ref, ...), custom_call_target="tpu_custom_call" | custom-call | flops 1073741824 | bytes 6291456 | tf_op jit(solution)/shard_map/pallas_call | solution.py:143
  50.4 12.4 %all_to_all.15.packet_ref = bf16[16,8,384]{2,1,0:T(8,128)(2,1)S(1)} all-to-all(bf16[16,8,384]{2,1,0:T(8,128)(2,1)S(1)} %shard_map.85), channel_id=1, replica_groups=mesh['zlo'=4,'x'=4,'y'=8,'zhi'=2,'core'=2] {'zlo','zhi','core'}, dimensions={0} | all-to-all | bytes 196608 | tf_op jit(solution)/shard_map/all_to_all | solution.py:195
  62.8 0.3 shard_map.86
  63.2 16.2 %all_to_all.16 = bf16[32,2,256]{2,1,0:T(2,128)(2,1)S(1)} all-to-all(bf16[32,2,256]{2,1,0:T(2,128)(2,1)S(1)} %reshape.7), channel_id=1, replica_groups=mesh['zlo'=4,'x'=4,'y'=8,'zhi'=2,'core'=2] {'x','y'}, dimensions={0} | all-to-all | bytes 65536 | tf_op jit(solution)/shard_map/all_to_all | solution.py:197
  79.3 0.6 convert_reduce_fusion
  (1 shorter events, 0.0 us)
Async XLA Ops:
  1.6 46.2 %copy-start.3 = (bf16[8,128,128]{2,1,0:T(8,128)(2,1)S(1)}, bf16[8,128,128]{2,1,0:T(8,128)(2,1)}, u32[]{:S(2)}) copy-start(bf16[8,128,128]{2,1,0:T(8,128)(2,1)} %stiffness_ref.1) | copy-start | bytes 786436
  1.6 46.2 %copy-start.5 = (s32[8]{0:T(128)S(1)}, s32[8]{0:T(128)}, u32[]{:S(2)}) copy-start(s32[8]{0:T(128)} %partner_ref.1) | copy-start | bytes 100
  1.6 37.3 %all-to-all-start = ((bf16[16,8,2048]{2,1,0:T(8,128)(2,1)}), bf16[16,8,2048]{2,1,0:T(8,128)(2,1)S(1)}, u32[]{:S(2)}, u32[]{:S(2)}) async-start(bf16[16,8,2048]{2,1,0:T(8,128)(2,1)} %shard_map.82), calls=%async_computation | async-start | bytes 1048576 | tf_op jit(solution)/shard_map/all_to_all | solution.py:187
  18.0 1.1 %copy-start.2 = (bf16[1024,400]{0,1:T(8,128)(2,1)S(1)}, bf16[1024,400]{0,1:T(8,128)(2,1)}, u32[]{:S(2)}) copy-start(bf16[1024,400]{0,1:T(8,128)(2,1)} %param.8) | copy-start | bytes 2457604
  19.1 0.7 copy-start.4
  19.8 0.7 copy-start.6
  21.4 1.0 %copy-start = (bf16[1024,512]{1,0:T(8,128)(2,1)}, bf16[1024,512]{1,0:T(8,128)(2,1)S(1)}, u32[]{:S(2)}) copy-start(bf16[1024,512]{1,0:T(8,128)(2,1)S(1)} %get-tuple-element.15.phi_ref) | copy-start | bytes 3145732
  39.0 3.5 %copy-start.7 = (bf16[16,8,2048]{2,1,0:T(8,128)(2,1)}, bf16[16,8,2048]{2,1,0:T(8,128)(2,1)S(1)}, u32[]{:S(2)}) copy-start(bf16[16,8,2048]{2,1,0:T(8,128)(2,1)S(1)} %all-to-all-done) | copy-start | bytes 1572868
  39.0 8.9 %copy-start.1 = (bf16[1024,512]{1,0:T(8,128)(2,1)S(1)}, bf16[1024,512]{1,0:T(8,128)(2,1)}, u32[]{:S(2)}) copy-start(bf16[1024,512]{1,0:T(8,128)(2,1)} %copy-done) | copy-start | bytes 3145732
  39.0 8.9 %collective-permute-start = (bf16[128,2048]{1,0:T(8,128)(2,1)S(1)}, bf16[128,2048]{1,0:T(8,128)(2,1)S(1)}, u32[]{:S(2)}, u32[]{:S(2)}) collective-permute-start(bf16[128,2048]{1,0:T(8,128)(2,1)S(1)} %bitcast.5), channel_id=1, source_target_pairs={{0,1},{1,0},{2,3},{3,2},{4,5},{5,4},{6,7},{7,6},{8,9},{9,8},{10,11... | collective-permute-start | bytes 1572872 | tf_op jit(solution)/shard_map/ppermute | solution.py:191

commit v3 on v2

--- a/solution.py
+++ b/solution.py
@@ -7,6 +7,12 @@
 
 AXES = ("zlo", "x", "y", "zhi", "core")
 SIZES = (4, 4, 8, 2, 2)
+SIZE = dict(zip(AXES, SIZES))
+SLOT_STEP = {"zlo": 256, "x": 64, "y": 8, "zhi": 4, "core": 2}
+FIRST = ("x", "core")
+SECOND = ("zlo", "y", "zhi")
+N_FIRST = 8
+N_SECOND = 64
 N_ROW = 32
 NT = (((1,), (1,)), ((), ()))
 TN = (((0,), (0,)), ((), ()))
@@ -65,10 +71,9 @@
     )(elem_zone, owner_slot, phi_t)
 
 
-def own_shapes_kernel(own_ref, phi_ref, psi_ref, shapes_ref, kept_ref, arrived):
-    rows, nc = psi_ref.shape
+def fetch_kernel(psi_ref, kept_ref, arrived):
     chunks = arrived.shape[0]
-    step = rows // chunks
+    step = psi_ref.shape[0] // chunks
     parts = [pl.ds(i * step, step) for i in range(chunks)]
     copies = [
         pltpu.make_async_copy(psi_ref.at[part], kept_ref.at[part], arrived.at[i])
@@ -76,48 +81,37 @@
     ]
     for copy in copies:
         copy.start()
-    for part, copy in zip(parts, copies):
-        total = lax.dot_general(
-            phi_ref[part], own_ref[:, nc:], NT, preferred_element_type=jnp.float32
-        )
+    for copy in copies:
         copy.wait()
-        total = total + lax.dot_general(
-            kept_ref[part], own_ref[:, :nc], NT, preferred_element_type=jnp.float32
-        )
-        shapes_ref[part] = total.astype(shapes_ref.dtype)
-
-
-def own_shapes(own, phi, psi, chunks=4):
-    rows, nc = psi.shape
-    return pl.pallas_call(
-        own_shapes_kernel,
-        out_shape=(
-            pltpu.VMEM((rows, own.shape[0]), jnp.bfloat16),
-            pltpu.VMEM((rows, nc), psi.dtype),
-        ),
-        in_specs=[VMEM, VMEM, pl.BlockSpec(memory_space=pltpu.HBM)],
-        out_specs=(VMEM, VMEM),
+
+
+def fetched(psi, chunks=4):
+    return pl.pallas_call(
+        fetch_kernel,
+        out_shape=pltpu.VMEM(psi.shape, psi.dtype),
+        in_specs=[pl.BlockSpec(memory_space=pltpu.HBM)],
+        out_specs=VMEM,
         scratch_shapes=[pltpu.SemaphoreType.DMA((chunks,))],
-        compiler_params=pltpu.CompilerParams(vmem_limit_bytes=52 * 2**20),
-        cost_estimate=pl.CostEstimate(flops=2**29, bytes_accessed=5 * 2**20, transcendentals=0),
-    )(own, phi, psi)
+        compiler_params=pltpu.CompilerParams(vmem_limit_bytes=57 * 2**20),
+        cost_estimate=pl.CostEstimate(flops=0, bytes_accessed=6 * 2**20, transcendentals=0),
+    )(psi)
 
 
 def energy_kernel(
-    partner_ref, other_ref, phi_ref, psi_ref, own_shapes_ref, stiffness_ref, codes_ref, out_ref, shapes
+    partner_ref, own_ref, other_ref, phi_ref, psi_ref, stiffness_ref, codes_ref, out_ref, coords, shapes
 ):
     half = other_ref.shape[0]
     nc = psi_ref.shape[1]
     nblocks, block, _ = stiffness_ref.shape
     modes = 2 * half
-    total = lax.dot_general(phi_ref[...], other_ref[:, nc:], NT, preferred_element_type=jnp.float32)
+    coords[:half] = own_ref[...]
+    coords[half:] = other_ref[...]
+    total = lax.dot_general(psi_ref[...], coords[:, :nc], NT, preferred_element_type=jnp.float32)
     total = total + lax.dot_general(
-        psi_ref[...], other_ref[:, :nc], NT, preferred_element_type=jnp.float32
+        phi_ref[...], coords[:, nc:], NT, preferred_element_type=jnp.float32
     )
     for b in range(nblocks):
-        part = slice(b * block, (b + 1) * block)
-        shapes[b, :, :half] = own_shapes_ref[part]
-        shapes[b, :, half:] = total[part].astype(shapes.dtype)
+        shapes[b] = total[b * block : (b + 1) * block].astype(shapes.dtype)
     sums = []
     for b in range(nblocks):
         own = shapes[b].astype(jnp.float32)
@@ -137,7 +131,7 @@
         out_ref[i, :, modes:] = codes_ref[...]
 
 
-def block_energy(partner, other, phi, psi, shapes, stiffness, codes, copies):
+def block_energy(partner, own, other, phi, psi, stiffness, codes, copies):
     nblocks, block, _ = stiffness.shape
     modes = 2 * other.shape[0]
     return pl.pallas_call(
@@ -145,10 +139,13 @@
         out_shape=jax.ShapeDtypeStruct((copies, nblocks, modes + CODE_LANES), jnp.bfloat16),
         in_specs=[SMEM, VMEM, VMEM, VMEM, VMEM, VMEM, VMEM],
         out_specs=VMEM,
-        scratch_shapes=[pltpu.VMEM((nblocks, block, modes), jnp.bfloat16)],
+        scratch_shapes=[
+            pltpu.VMEM((modes, own.shape[1]), jnp.bfloat16),
+            pltpu.VMEM((nblocks, block, modes), jnp.bfloat16),
+        ],
         compiler_params=pltpu.CompilerParams(vmem_limit_bytes=24 * 2**20),
         cost_estimate=pl.CostEstimate(flops=2**30, bytes_accessed=6 * 2**20, transcendentals=0),
-    )(partner, other, phi, psi, shapes, stiffness, codes)
+    )(partner, own, other, phi, psi, stiffness, codes)
 
 
 def zone_kernel(packet_ref, out_ref):
@@ -157,9 +154,12 @@
     packet = packet_ref[...].astype(jnp.float32).reshape(peers * nblocks, width)
     slot = packet[:, modes : modes + 1] * 32.0 + packet[:, modes + 1 : modes + 2]
     place = lax.broadcasted_iota(jnp.int32, (1, out_ref.shape[0]), 1)
-    corner = lax.axis_index("zlo") * 256 + lax.axis_index("zhi") * 4 + lax.axis_index("core") * 2
-    owned = (corner + place // 2 * 8 + place % 2).astype(jnp.float32)
-    chosen = (slot == owned).astype(jnp.float32).astype(jnp.bfloat16)
+    owned = place % 2 + sum(SLOT_STEP[axis] * lax.axis_index(axis) for axis in FIRST)
+    peer = place // 2
+    for axis in reversed(SECOND):
+        owned = owned + peer % SIZE[axis] * SLOT_STEP[axis]
+        peer = peer // SIZE[axis]
+    chosen = (slot == owned.astype(jnp.float32)).astype(jnp.float32).astype(jnp.bfloat16)
     energy = packet[:, :modes].astype(jnp.bfloat16)
     sums = lax.dot_general(chosen, energy, TN, preferred_element_type=jnp.float32)
     out_ref[...] = sums.astype(out_ref.dtype)
@@ -190,11 +190,11 @@
     own, phi, codes = lax.optimization_barrier((own, phi, codes))
     other = lax.ppermute(own, "core", [(0, 1), (1, 0)])
 
-    shapes, psi = own_shapes(own, phi, psi_rows)
-    energy = block_energy(partner, other, phi, psi, shapes, stiffness, codes, 16)
-    along_z = lax.all_to_all(energy, ("zlo", "zhi", "core"), 0, 0, tiled=True)
-    partial_sums = zone_sums(along_z, 64).reshape(32, 2, modes)
-    received = lax.all_to_all(partial_sums, ("x", "y"), 0, 0, tiled=True)
+    psi = fetched(psi_rows)
+    energy = block_energy(partner, own, other, phi, psi, stiffness, codes, N_FIRST)
+    gathered = lax.all_to_all(energy, FIRST, 0, 0, tiled=True)
+    partial_sums = zone_sums(gathered, 2 * N_SECOND).reshape(N_SECOND, 2, modes)
+    received = lax.all_to_all(partial_sums, SECOND, 0, 0, tiled=True)
     return jnp.sum(received.astype(jnp.float32), axis=0)
 
 

time: 80.5 us -> 76.2 us (0.947)
  Pallas kernels: 10.8 us -> 7.28 us
  waiting for transfers between devices: 16.6 us -> 17.6 us
  local copies, waits for them, and re-layouts: 3.49 us -> 2.53 us
    pallas_call x1, Pallas kernels: 5.39 us -> 1.88 us  [fetched(): pl.pallas_call(fetch_kernel, out_shape=pltpu.VMEM(psi.shape, psi.dtype),...]
    unnamed x16 -> x10, local copies, waits for them, and re-layouts: 3.46 us -> 2.49 us
    all_to_all x1, waiting for transfers between devices: 16.6 us -> 17.6 us  [on_device(): lax.all_to_all(sent, ('y', 'zhi'), 0, 0, tiled=True)]
  transfers between devices with their start and end apart: 2 -> 2, of which waited for: 1 -> 1; matrix products, arithmetic and copies ran while one was open for 0% -> 0% of each run, Pallas kernels for 8% -> 4%
where the time goes in v3:
time: 76.2 us; the launch traced here: 75.7 us
  blocking collectives  27.9 us (37%)
  starting transfers between devices  19.6 us (26%)
  waiting for transfers between devices  17.6 us (23%)
  Pallas kernels  7.28 us (10%)
  local copies, waits for them, and re-layouts  2.53 us (3%)
    all_to_all x1, blocking collectives, on_device(): received = lax.all_to_all(partial_sums, SECOND, 0, 0, tiled=True)  18.9 us
    all_to_all x1, waiting for transfers between devices, on_device(): lax.all_to_all(sent, ('y', 'zhi'), 0, 0, tiled=True)  17.6 us
    all_to_all x1, starting transfers between devices, on_device(): lax.all_to_all(sent, ('y', 'zhi'), 0, 0, tiled=True)  16.2 us
    all_to_all x1, blocking collectives, on_device(): gathered = lax.all_to_all(energy, FIRST, 0, 0, tiled=True)  8.98 us
    ppermute x1, starting transfers between devices, on_device(): other = lax.ppermute(own, 'core', [(0, 1), (1, 0)])  3.45 us
    pallas_call x1, Pallas kernels, block_energy(): pl.pallas_call(energy_kernel, out_shape=jax.ShapeDtypeStruct((copies, nbl...  2.55 us
    unnamed x10, local copies, waits for them, and re-layouts  2.49 us
    pallas_call x1, Pallas kernels, fetched(): pl.pallas_call(fetch_kernel, out_shape=pltpu.VMEM(psi.shape, psi.dtype),...  1.88 us
  transfers between devices with their start and end apart: 2, of which 1 were waited for; matrix products, arithmetic and copies ran while one was open for 0% of the time, Pallas kernels for 4%

profile of v3, /device:TPU:1, one launch (start us, length us, event | category | flops | bytes accessed | tf_op | source)
XLA Modules:
  0.0 75.7 jit_solution(14413693566035328831)
XLA Ops:
  0.0 1.6 %shard_map.82 = bf16[16,8,2048]{2,1,0:T(8,128)(2,1)} custom-call(bf16[8,1536]{1,0:T(8,128)(2,1)} %bitcast.7, bf16[8,400]{1,0:T(8,128)(2,1)} %bitcast.8), custom_call_target="tpu_custom_call" | custom-call | tf_op jit(solution)/shard_map/pallas_call | solution.py:37
  1.6 16.2 %all-to-all-start = ((bf16[16,8,2048]{2,1,0:T(8,128)(2,1)}), bf16[16,8,2048]{2,1,0:T(8,128)(2,1)S(1)}, u32[]{:S(2)}, u32[]{:S(2)}) async-start(bf16[16,8,2048]{2,1,0:T(8,128)(2,1)} %shard_map.82), calls=%async_computation | async-start | bytes 1048576 | tf_op jit(solution)/shard_map/all_to_all | solution.py:187
  17.8 0.0 copy-start
  17.8 1.1 %copy-done = bf16[1024,400]{0,1:T(8,128)(2,1)S(1)} copy-done((bf16[1024,400]{0,1:T(8,128)(2,1)S(1)}, bf16[1024,400]{0,1:T(8,128)(2,1)}, u32[]{:S(2)}) %copy-start) | copy-done | bytes 819224
  18.9 0.0 copy-start.2
  18.9 0.7 copy-done.2
  19.6 0.0 copy-start.3
  19.6 0.7 copy-done.3
  20.3 0.9 %shard_map.83 = (bf16[1024,512]{1,0:T(8,128)(2,1)S(1)}, bf16[8,128]{1,0:T(8,128)(2,1)S(1)}) custom-call(s32[8]{0:T(128)S(1)} %copy-done.3, s32[1024]{0:T(1024)S(1)} %copy-done.2, bf16[400,1024]{1,0:T(8,128)(2,1)S(1)} %bitcast.6), custom_call_target="tpu_custom_call" | custom-call | bytes 8388608 | tf_op jit(solution)/shard_map/pallas_call | solution.py:61
  21.2 17.6 %all-to-all-done = bf16[16,8,2048]{2,1,0:T(8,128)(2,1)S(1)} async-done(((bf16[16,8,2048]{2,1,0:T(8,128)(2,1)}), bf16[16,8,2048]{2,1,0:T(8,128)(2,1)S(1)}, u32[]{:S(2)}, u32[]{:S(2)}) %all-to-all-start) | async-done | bytes 524320 | tf_op jit(solution)/shard_map/all_to_all | solution.py:187
  38.8 0.0 copy-start.1
  38.8 0.0 copy-start.4
  38.8 3.4 %collective-permute-start = (bf16[128,2048]{1,0:T(8,128)(2,1)S(1)}, bf16[128,2048]{1,0:T(8,128)(2,1)S(1)}, u32[]{:S(2)}, u32[]{:S(2)}) collective-permute-start(bf16[128,2048]{1,0:T(8,128)(2,1)S(1)} %bitcast.4), channel_id=1, source_target_pairs={{0,1},{1,0},{2,3},{3,2},{4,5},{5,4},{6,7},{7,6},{8,9},{9,8},{10,11... | collective-permute-start | bytes 1572872 | tf_op jit(solution)/shard_map/ppermute | solution.py:191
  42.3 1.9 %shard_map.84.psi_ref = bf16[1024,1536]{1,0:T(8,128)(2,1)S(1)} custom-call(bf16[1024,1536]{1,0:T(8,128)(2,1)} %psi_ref.1), custom_call_target="tpu_custom_call" | custom-call | bytes 6291456 | tf_op jit(solution)/shard_map/pallas_call | solution.py:89
  44.1 0.0 collective-permute-done.other_ref
  44.2 0.0 copy-done.1
  44.2 0.0 copy-done.4
  44.2 2.6 %shard_map.85 = bf16[8,8,384]{2,1,0:T(8,128)(2,1)S(1)} custom-call(s32[8]{0:T(128)S(1)} %copy-done.4, bf16[128,2048]{1,0:T(8,128)(2,1)S(1)} %bitcast.5, bf16[128,2048]{1,0:T(8,128)(2,1)S(1)} %collective-permute-done.other_ref, bf16[1024,512]{1,0:T(8,128)(2,1)S(1)} %get-tuple-element.13.phi_ref, bf16[1024,1536]{1,0:T(8,128)(2,1)S(1)} %shard_map.84.psi_ref, ...), custom_call_target="tpu_custom_call" | custom-call | flops 1073741824 | bytes 6291456 | tf_op jit(solution)/shard_map/pallas_call | solution.py:137
  46.7 9.0 %all_to_all.15.packet_ref = bf16[8,8,384]{2,1,0:T(8,128)(2,1)S(1)} all-to-all(bf16[8,8,384]{2,1,0:T(8,128)(2,1)S(1)} %shard_map.85), channel_id=1, replica_groups=mesh['zlo'=4,'x'=4,'y'=8,'zhi'=2,'core'=2] {'x','core'}, dimensions={0} | all-to-all | bytes 98304 | tf_op jit(solution)/shard_map/all_to_all | solution.py:195
  55.7 0.3 shard_map.86
  56.1 18.9 %all_to_all.16 = bf16[64,2,256]{2,1,0:T(2,128)(2,1)S(1)} all-to-all(bf16[64,2,256]{2,1,0:T(2,128)(2,1)S(1)} %reshape.7), channel_id=1, replica_groups=mesh['zlo'=4,'x'=4,'y'=8,'zhi'=2,'core'=2] {'zlo','y','zhi'}, dimensions={0} | all-to-all | bytes 131072 | tf_op jit(solution)/shard_map/all_to_all | solution.py:197
  75.0 0.7 convert_reduce_fusion
  (1 shorter events, 0.0 us)
Async XLA Ops:
  1.6 37.2 %all-to-all-start = ((bf16[16,8,2048]{2,1,0:T(8,128)(2,1)}), bf16[16,8,2048]{2,1,0:T(8,128)(2,1)S(1)}, u32[]{:S(2)}, u32[]{:S(2)}) async-start(bf16[16,8,2048]{2,1,0:T(8,128)(2,1)} %shard_map.82), calls=%async_computation | async-start | bytes 1048576 | tf_op jit(solution)/shard_map/all_to_all | solution.py:187
  17.8 1.1 %copy-start = (bf16[1024,400]{0,1:T(8,128)(2,1)S(1)}, bf16[1024,400]{0,1:T(8,128)(2,1)}, u32[]{:S(2)}) copy-start(bf16[1024,400]{0,1:T(8,128)(2,1)} %param.8) | copy-start | bytes 2457604
  18.9 0.7 copy-start.2
  19.6 0.7 copy-start.3
  38.8 5.4 %copy-start.1 = (bf16[8,128,128]{2,1,0:T(8,128)(2,1)S(1)}, bf16[8,128,128]{2,1,0:T(8,128)(2,1)}, u32[]{:S(2)}) copy-start(bf16[8,128,128]{2,1,0:T(8,128)(2,1)} %stiffness_ref.1) | copy-start | bytes 786436
  38.8 5.4 %copy-start.4 = (s32[8]{0:T(128)S(1)}, s32[8]{0:T(128)}, u32[]{:S(2)}) copy-start(s32[8]{0:T(128)} %partner_ref.1) | copy-start | bytes 100
  38.8 5.3 %collective-permute-start = (bf16[128,2048]{1,0:T(8,128)(2,1)S(1)}, bf16[128,2048]{1,0:T(8,128)(2,1)S(1)}, u32[]{:S(2)}, u32[]{:S(2)}) collective-permute-start(bf16[128,2048]{1,0:T(8,128)(2,1)S(1)} %bitcast.4), channel_id=1, source_target_pairs={{0,1},{1,0},{2,3},{3,2},{4,5},{5,4},{6,7},{7,6},{8,9},{9,8},{10,11... | collective-permute-start | bytes 1572872 | tf_op jit(solution)/shard_map/ppermute | solution.py:191

commit v4 on v3

--- a/solution.py
+++ b/solution.py
@@ -123,7 +123,8 @@
     source = lax.broadcasted_iota(jnp.int32, (modes, modes), 0)
     target = lax.broadcasted_iota(jnp.int32, (modes, modes), 1)
     core = (source // half + lax.axis_index("core")) % 2
-    ordered = (source % half) // 8 * 16 + core * 8 + source % 8
+    peer = (source % half) // 8
+    ordered = peer % 8 * 32 + peer // 8 * 16 + core * 8 + source % 8
     move = (ordered == target).astype(jnp.float32).astype(jnp.bfloat16)
     energy = jnp.dot(energy, move, preferred_element_type=jnp.float32).astype(jnp.bfloat16)
     for i in range(out_ref.shape[0]):
@@ -184,7 +185,7 @@
     width = nc + nf + -(nc + nf) % 128
 
     sent = packets(coord_con[0], coord_fixed[0], N_ROW // 2, width)
-    own = lax.all_to_all(sent, ("y", "zhi"), 0, 0, tiled=True).reshape(modes // 2, width)
+    own = lax.all_to_all(sent, ("zhi", "y"), 0, 0, tiled=True).reshape(modes // 2, width)
 
     phi, codes = early(elem_zone, owner_slot, phi_rows.T, width - nc)
     own, phi, codes = lax.optimization_barrier((own, phi, codes))

time: 76.2 us -> 73.8 us (0.969)
  waiting for transfers between devices: 17.6 us -> 14.7 us
  starting transfers between devices: 19.6 us -> 20.7 us
    all_to_all x1, waiting for transfers between devices: 17.6 us -> 14.7 us  [on_device(): lax.all_to_all(sent, ('zhi', 'y'), 0, 0, tiled=True)]
    ppermute x1, starting transfers between devices: 3.45 us -> 4.51 us  [on_device(): other = lax.ppermute(own, 'core', [(0, 1), (1, 0)])]
where the time goes in v4:
time: 73.8 us; the launch traced here: 73.3 us
  blocking collectives  27.4 us (37%)
  starting transfers between devices  20.7 us (28%)
  waiting for transfers between devices  14.7 us (20%)
  Pallas kernels  7.33 us (10%)
  local copies, waits for them, and re-layouts  2.53 us (3%)
    all_to_all x1, blocking collectives, on_device(): received = lax.all_to_all(partial_sums, SECOND, 0, 0, tiled=True)  18.4 us
    all_to_all x1, starting transfers between devices, on_device(): lax.all_to_all(sent, ('zhi', 'y'), 0, 0, tiled=True)  16.2 us
    all_to_all x1, waiting for transfers between devices, on_device(): lax.all_to_all(sent, ('zhi', 'y'), 0, 0, tiled=True)  14.7 us
    all_to_all x1, blocking collectives, on_device(): gathered = lax.all_to_all(energy, FIRST, 0, 0, tiled=True)  8.99 us
    ppermute x1, starting transfers between devices, on_device(): other = lax.ppermute(own, 'core', [(0, 1), (1, 0)])  4.51 us
    pallas_call x1, Pallas kernels, block_energy(): pl.pallas_call(energy_kernel, out_shape=jax.ShapeDtypeStruct((copies, nbl...  2.6 us
    unnamed x10, local copies, waits for them, and re-layouts  2.49 us
    pallas_call x1, Pallas kernels, fetched(): pl.pallas_call(fetch_kernel, out_shape=pltpu.VMEM(psi.shape, psi.dtype),...  1.88 us
  transfers between devices with their start and end apart: 2, of which 1 were waited for; matrix products, arithmetic and copies ran while one was open for 0% of the time, Pallas kernels for 4%

profile of v4, /device:TPU:1, one launch (start us, length us, event | category | flops | bytes accessed | tf_op | source)
XLA Modules:
  0.0 73.3 jit_solution(15418349102675852095)
XLA Ops:
  0.0 1.6 %shard_map.82 = bf16[16,8,2048]{2,1,0:T(8,128)(2,1)} custom-call(bf16[8,1536]{1,0:T(8,128)(2,1)} %bitcast.7, bf16[8,400]{1,0:T(8,128)(2,1)} %bitcast.8), custom_call_target="tpu_custom_call" | custom-call | tf_op jit(solution)/shard_map/pallas_call | solution.py:37
  1.6 16.2 %all-to-all-start = ((bf16[16,8,2048]{2,1,0:T(8,128)(2,1)}), bf16[16,8,2048]{2,1,0:T(8,128)(2,1)S(1)}, u32[]{:S(2)}, u32[]{:S(2)}) async-start(bf16[16,8,2048]{2,1,0:T(8,128)(2,1)} %shard_map.82), calls=%async_computation | async-start | bytes 1048576 | tf_op jit(solution)/shard_map/all_to_all | solution.py:188
  17.8 0.0 copy-start
  17.8 1.1 %copy-done = bf16[1024,400]{0,1:T(8,128)(2,1)S(1)} copy-done((bf16[1024,400]{0,1:T(8,128)(2,1)S(1)}, bf16[1024,400]{0,1:T(8,128)(2,1)}, u32[]{:S(2)}) %copy-start) | copy-done | bytes 819224
  18.9 0.0 copy-start.2
  18.9 0.7 copy-done.2
  19.6 0.0 copy-start.3
  19.6 0.7 copy-done.3
  20.3 0.9 %shard_map.83 = (bf16[1024,512]{1,0:T(8,128)(2,1)S(1)}, bf16[8,128]{1,0:T(8,128)(2,1)S(1)}) custom-call(s32[8]{0:T(128)S(1)} %copy-done.3, s32[1024]{0:T(1024)S(1)} %copy-done.2, bf16[400,1024]{1,0:T(8,128)(2,1)S(1)} %bitcast.6), custom_call_target="tpu_custom_call" | custom-call | bytes 8388608 | tf_op jit(solution)/shard_map/pallas_call | solution.py:61
  21.2 14.7 %all-to-all-done = bf16[16,8,2048]{2,1,0:T(8,128)(2,1)S(1)} async-done(((bf16[16,8,2048]{2,1,0:T(8,128)(2,1)}), bf16[16,8,2048]{2,1,0:T(8,128)(2,1)S(1)}, u32[]{:S(2)}, u32[]{:S(2)}) %all-to-all-start) | async-done | bytes 524320 | tf_op jit(solution)/shard_map/all_to_all | solution.py:188
  35.9 0.0 copy-start.1
  35.9 0.0 copy-start.4
  35.9 4.5 %collective-permute-start = (bf16[128,2048]{1,0:T(8,128)(2,1)S(1)}, bf16[128,2048]{1,0:T(8,128)(2,1)S(1)}, u32[]{:S(2)}, u32[]{:S(2)}) collective-permute-start(bf16[128,2048]{1,0:T(8,128)(2,1)S(1)} %bitcast.4), channel_id=1, source_target_pairs={{0,1},{1,0},{2,3},{3,2},{4,5},{5,4},{6,7},{7,6},{8,9},{9,8},{10,11... | collective-permute-start | bytes 1572872 | tf_op jit(solution)/shard_map/ppermute | solution.py:192
  40.4 1.9 %shard_map.84.psi_ref = bf16[1024,1536]{1,0:T(8,128)(2,1)S(1)} custom-call(bf16[1024,1536]{1,0:T(8,128)(2,1)} %psi_ref.1), custom_call_target="tpu_custom_call" | custom-call | bytes 6291456 | tf_op jit(solution)/shard_map/pallas_call | solution.py:89
  42.3 0.0 collective-permute-done.other_ref
  42.3 0.0 copy-done.1
  42.3 0.0 copy-done.4
  42.3 2.6 %shard_map.85 = bf16[8,8,384]{2,1,0:T(8,128)(2,1)S(1)} custom-call(s32[8]{0:T(128)S(1)} %copy-done.4, bf16[128,2048]{1,0:T(8,128)(2,1)S(1)} %bitcast.5, bf16[128,2048]{1,0:T(8,128)(2,1)S(1)} %collective-permute-done.other_ref, bf16[1024,512]{1,0:T(8,128)(2,1)S(1)} %get-tuple-element.13.phi_ref, bf16[1024,1536]{1,0:T(8,128)(2,1)S(1)} %shard_map.84.psi_ref, ...), custom_call_target="tpu_custom_call" | custom-call | flops 1073741824 | bytes 6291456 | tf_op jit(solution)/shard_map/pallas_call | solution.py:138
  44.9 9.0 %all_to_all.15.packet_ref = bf16[8,8,384]{2,1,0:T(8,128)(2,1)S(1)} all-to-all(bf16[8,8,384]{2,1,0:T(8,128)(2,1)S(1)} %shard_map.85), channel_id=1, replica_groups=mesh['zlo'=4,'x'=4,'y'=8,'zhi'=2,'core'=2] {'x','core'}, dimensions={0} | all-to-all | bytes 98304 | tf_op jit(solution)/shard_map/all_to_all | solution.py:196
  53.9 0.3 shard_map.86
  54.3 18.4 %all_to_all.16 = bf16[64,2,256]{2,1,0:T(2,128)(2,1)S(1)} all-to-all(bf16[64,2,256]{2,1,0:T(2,128)(2,1)S(1)} %reshape.7), channel_id=1, replica_groups=mesh['zlo'=4,'x'=4,'y'=8,'zhi'=2,'core'=2] {'zlo','y','zhi'}, dimensions={0} | all-to-all | bytes 131072 | tf_op jit(solution)/shard_map/all_to_all | solution.py:198
  72.7 0.7 convert_reduce_fusion
  (1 shorter events, 0.0 us)
Async XLA Ops:
  1.6 34.3 %all-to-all-start = ((bf16[16,8,2048]{2,1,0:T(8,128)(2,1)}), bf16[16,8,2048]{2,1,0:T(8,128)(2,1)S(1)}, u32[]{:S(2)}, u32[]{:S(2)}) async-start(bf16[16,8,2048]{2,1,0:T(8,128)(2,1)} %shard_map.82), calls=%async_computation | async-start | bytes 1048576 | tf_op jit(solution)/shard_map/all_to_all | solution.py:188
  17.8 1.1 %copy-start = (bf16[1024,400]{0,1:T(8,128)(2,1)S(1)}, bf16[1024,400]{0,1:T(8,128)(2,1)}, u32[]{:S(2)}) copy-start(bf16[1024,400]{0,1:T(8,128)(2,1)} %param.8) | copy-start | bytes 2457604
  18.9 0.7 copy-start.2
  19.6 0.7 copy-start.3
  35.9 6.4 %copy-start.1 = (bf16[8,128,128]{2,1,0:T(8,128)(2,1)S(1)}, bf16[8,128,128]{2,1,0:T(8,128)(2,1)}, u32[]{:S(2)}) copy-start(bf16[8,128,128]{2,1,0:T(8,128)(2,1)} %stiffness_ref.1) | copy-start | bytes 786436
  35.9 6.4 %copy-start.4 = (s32[8]{0:T(128)S(1)}, s32[8]{0:T(128)}, u32[]{:S(2)}) copy-start(s32[8]{0:T(128)} %partner_ref.1) | copy-start | bytes 100
  35.9 6.4 %collective-permute-start = (bf16[128,2048]{1,0:T(8,128)(2,1)S(1)}, bf16[128,2048]{1,0:T(8,128)(2,1)S(1)}, u32[]{:S(2)}, u32[]{:S(2)}) collective-permute-start(bf16[128,2048]{1,0:T(8,128)(2,1)S(1)} %bitcast.4), channel_id=1, source_target_pairs={{0,1},{1,0},{2,3},{3,2},{4,5},{5,4},{6,7},{7,6},{8,9},{9,8},{10,11... | collective-permute-start | bytes 1572872 | tf_op jit(solution)/shard_map/ppermute | solution.py:192

commit v5 on v4

--- a/solution.py
+++ b/solution.py
@@ -123,7 +123,7 @@
     source = lax.broadcasted_iota(jnp.int32, (modes, modes), 0)
     target = lax.broadcasted_iota(jnp.int32, (modes, modes), 1)
     core = (source // half + lax.axis_index("core")) % 2
-    peer = (source % half) // 8
+    peer = half // 8 - 1 - (source % half) // 8
     ordered = peer % 8 * 32 + peer // 8 * 16 + core * 8 + source % 8
     move = (ordered == target).astype(jnp.float32).astype(jnp.bfloat16)
     energy = jnp.dot(energy, move, preferred_element_type=jnp.float32).astype(jnp.bfloat16)
@@ -156,7 +156,7 @@
     slot = packet[:, modes : modes + 1] * 32.0 + packet[:, modes + 1 : modes + 2]
     place = lax.broadcasted_iota(jnp.int32, (1, out_ref.shape[0]), 1)
     owned = place % 2 + sum(SLOT_STEP[axis] * lax.axis_index(axis) for axis in FIRST)
-    peer = place // 2
+    peer = N_SECOND - 1 - place // 2
     for axis in reversed(SECOND):
         owned = owned + peer % SIZE[axis] * SLOT_STEP[axis]
         peer = peer // SIZE[axis]
@@ -176,6 +176,11 @@
     )(packet)
 
 
+def exchange(blocks, axes):
+    members = list(range(blocks.shape[0]))[::-1]
+    return lax.all_to_all(blocks, axes, 0, 0, axis_index_groups=[members], tiled=True)
+
+
 def on_device(
     phi_rows, psi_rows, stiffness, coord_fixed, coord_con, elem_zone, partner, owner_slot
 ):
@@ -185,7 +190,7 @@
     width = nc + nf + -(nc + nf) % 128
 
     sent = packets(coord_con[0], coord_fixed[0], N_ROW // 2, width)
-    own = lax.all_to_all(sent, ("zhi", "y"), 0, 0, tiled=True).reshape(modes // 2, width)
+    own = exchange(sent, ("zhi", "y")).reshape(modes // 2, width)
 
     phi, codes = early(elem_zone, owner_slot, phi_rows.T, width - nc)
     own, phi, codes = lax.optimization_barrier((own, phi, codes))
@@ -193,9 +198,9 @@
 
     psi = fetched(psi_rows)
     energy = block_energy(partner, own, other, phi, psi, stiffness, codes, N_FIRST)
-    gathered = lax.all_to_all(energy, FIRST, 0, 0, tiled=True)
+    gathered = exchange(energy, FIRST)
     partial_sums = zone_sums(gathered, 2 * N_SECOND).reshape(N_SECOND, 2, modes)
-    received = lax.all_to_all(partial_sums, SECOND, 0, 0, tiled=True)
+    received = exchange(partial_sums, SECOND)
     return jnp.sum(received.astype(jnp.float32), axis=0)
 
 

time: 73.8 us -> 66.8 us (0.905)
  waiting for transfers between devices: 14.7 us -> 9.72 us
  blocking collectives: 27.4 us -> 24.6 us
    all_to_all x1, waiting for transfers between devices: 14.7 us -> 9.72 us  [exchange(): lax.all_to_all(blocks, axes, 0, 0, axis_index_groups=[members], tiled=True)]
    all_to_all x2, blocking collectives: 27.4 us -> 24.6 us  [exchange(): lax.all_to_all(blocks, axes, 0, 0, axis_index_groups=[members], tiled=True)]
where the time goes in v5:
time: 66.8 us; the launch traced here: 66.2 us
  blocking collectives  24.6 us (37%)
  starting transfers between devices  21.3 us (32%)
  waiting for transfers between devices  9.72 us (15%)
  Pallas kernels  7.39 us (11%)
  local copies, waits for them, and re-layouts  2.53 us (4%)
  other arithmetic  0.67 us (1%)
    all_to_all x2, blocking collectives, exchange(): lax.all_to_all(blocks, axes, 0, 0, axis_index_groups=[members], tiled=True)  24.6 us
    all_to_all x1, starting transfers between devices, exchange(): lax.all_to_all(blocks, axes, 0, 0, axis_index_groups=[members], tiled=True)  16.4 us
    all_to_all x1, waiting for transfers between devices, exchange(): lax.all_to_all(blocks, axes, 0, 0, axis_index_groups=[members], tiled=True)  9.72 us
    ppermute x1, starting transfers between devices, on_device(): other = lax.ppermute(own, 'core', [(0, 1), (1, 0)])  4.86 us
    pallas_call x1, Pallas kernels, block_energy(): pl.pallas_call(energy_kernel, out_shape=jax.ShapeDtypeStruct((copies, nbl...  2.66 us
    unnamed x10, local copies, waits for them, and re-layouts  2.49 us
    pallas_call x1, Pallas kernels, fetched(): pl.pallas_call(fetch_kernel, out_shape=pltpu.VMEM(psi.shape, psi.dtype),...  1.88 us
    pallas_call x1, Pallas kernels, packets(): pl.pallas_call(packet_kernel, out_shape=jax.ShapeDtypeStruct((copies, con...  1.59 us
  transfers between devices with their start and end apart: 2, of which 1 were waited for; matrix products, arithmetic and copies ran while one was open for 0% of the time, Pallas kernels for 4%

profile of v5, /device:TPU:1, one launch (start us, length us, event | category | flops | bytes accessed | tf_op | source)
XLA Modules:
  0.0 66.2 jit_solution(498889979486329047)
XLA Ops:
  0.0 1.6 %shard_map.82 = bf16[16,8,2048]{2,1,0:T(8,128)(2,1)} custom-call(bf16[8,1536]{1,0:T(8,128)(2,1)} %bitcast.7, bf16[8,400]{1,0:T(8,128)(2,1)} %bitcast.8), custom_call_target="tpu_custom_call" | custom-call | tf_op jit(solution)/shard_map/pallas_call | solution.py:37
  1.6 16.4 %all-to-all-start = ((bf16[16,8,2048]{2,1,0:T(8,128)(2,1)}), bf16[16,8,2048]{2,1,0:T(8,128)(2,1)S(1)}, u32[]{:S(2)}, u32[]{:S(2)}) async-start(bf16[16,8,2048]{2,1,0:T(8,128)(2,1)} %shard_map.82), calls=%async_computation | async-start | bytes 1048576 | tf_op jit(solution)/shard_map/all_to_all | solution.py:181
  18.0 0.0 copy-start
  18.0 1.1 %copy-done = bf16[1024,400]{0,1:T(8,128)(2,1)S(1)} copy-done((bf16[1024,400]{0,1:T(8,128)(2,1)S(1)}, bf16[1024,400]{0,1:T(8,128)(2,1)}, u32[]{:S(2)}) %copy-start) | copy-done | bytes 819224
  19.1 0.0 copy-start.2
  19.1 0.7 %copy-done.2 = s32[1024]{0:T(1024)S(1)} copy-done((s32[1024]{0:T(1024)S(1)}, s32[1024]{0:T(1024)}, u32[]{:S(2)}) %copy-start.2) | copy-done | bytes 4120
  19.8 0.0 copy-start.3
  19.8 0.7 copy-done.3
  20.5 0.9 %shard_map.83 = (bf16[1024,512]{1,0:T(8,128)(2,1)S(1)}, bf16[8,128]{1,0:T(8,128)(2,1)S(1)}) custom-call(s32[8]{0:T(128)S(1)} %copy-done.3, s32[1024]{0:T(1024)S(1)} %copy-done.2, bf16[400,1024]{1,0:T(8,128)(2,1)S(1)} %bitcast.6), custom_call_target="tpu_custom_call" | custom-call | bytes 8388608 | tf_op jit(solution)/shard_map/pallas_call | solution.py:61
  21.4 9.7 %all-to-all-done = bf16[16,8,2048]{2,1,0:T(8,128)(2,1)S(1)} async-done(((bf16[16,8,2048]{2,1,0:T(8,128)(2,1)}), bf16[16,8,2048]{2,1,0:T(8,128)(2,1)S(1)}, u32[]{:S(2)}, u32[]{:S(2)}) %all-to-all-start) | async-done | bytes 524320 | tf_op jit(solution)/shard_map/all_to_all | solution.py:181
  31.1 0.0 copy-start.1
  31.1 0.0 copy-start.4
  31.1 4.9 %collective-permute-start = (bf16[128,2048]{1,0:T(8,128)(2,1)S(1)}, bf16[128,2048]{1,0:T(8,128)(2,1)S(1)}, u32[]{:S(2)}, u32[]{:S(2)}) collective-permute-start(bf16[128,2048]{1,0:T(8,128)(2,1)S(1)} %bitcast.4), channel_id=1, source_target_pairs={{0,1},{1,0},{2,3},{3,2},{4,5},{5,4},{6,7},{7,6},{8,9},{9,8},{10,11... | collective-permute-start | bytes 1572872 | tf_op jit(solution)/shard_map/ppermute | solution.py:197
  36.0 1.9 %shard_map.84.psi_ref = bf16[1024,1536]{1,0:T(8,128)(2,1)S(1)} custom-call(bf16[1024,1536]{1,0:T(8,128)(2,1)} %psi_ref.1), custom_call_target="tpu_custom_call" | custom-call | bytes 6291456 | tf_op jit(solution)/shard_map/pallas_call | solution.py:89
  37.9 0.0 collective-permute-done.other_ref
  37.9 0.0 copy-done.1
  37.9 0.0 copy-done.4
  37.9 2.7 %shard_map.85 = bf16[8,8,384]{2,1,0:T(8,128)(2,1)S(1)} custom-call(s32[8]{0:T(128)S(1)} %copy-done.4, bf16[128,2048]{1,0:T(8,128)(2,1)S(1)} %bitcast.5, bf16[128,2048]{1,0:T(8,128)(2,1)S(1)} %collective-permute-done.other_ref, bf16[1024,512]{1,0:T(8,128)(2,1)S(1)} %get-tuple-element.13.phi_ref, bf16[1024,1536]{1,0:T(8,128)(2,1)S(1)} %shard_map.84.psi_ref, ...), custom_call_target="tpu_custom_call" | custom-call | flops 1073741824 | bytes 6291456 | tf_op jit(solution)/shard_map/pallas_call | solution.py:138
  40.6 7.8 %all_to_all.15.packet_ref = bf16[8,8,384]{2,1,0:T(8,128)(2,1)S(1)} all-to-all(bf16[8,8,384]{2,1,0:T(8,128)(2,1)S(1)} %shard_map.85), channel_id=1, replica_groups={{97,96,65,64,33,32,1,0},{99,98,67,66,35,34,3,2},{101,100,69,68,37,36,5,..., dimensions={0} | all-to-all | bytes 98304 | tf_op jit(solution)/shard_map/all_to_all | solution.py:181
  48.4 0.3 shard_map.86
  48.8 16.7 %all_to_all.16 = bf16[64,2,256]{2,1,0:T(2,128)(2,1)S(1)} all-to-all(bf16[64,2,256]{2,1,0:T(2,128)(2,1)S(1)} %reshape.7), channel_id=1, replica_groups={{414,412,410,408,406,404,402,400,398,396,394,392,390,388,386,384,286,28..., dimensions={0} | all-to-all | bytes 131072 | tf_op jit(solution)/shard_map/all_to_all | solution.py:181
  65.5 0.7 %convert_reduce_fusion = f32[2,256]{1,0:T(2,128)} fusion(bf16[64,2,256]{2,1,0:T(2,128)(2,1)S(1)} %all_to_all.16), kind=kLoop, calls=%fused_computation | loop fusion | flops 65024 | bytes 67584 | tf_op jit(solution)/shard_map/reduce_sum | solution.py:204
  (1 shorter events, 0.0 us)
Async XLA Ops:
  1.6 29.5 %all-to-all-start = ((bf16[16,8,2048]{2,1,0:T(8,128)(2,1)}), bf16[16,8,2048]{2,1,0:T(8,128)(2,1)S(1)}, u32[]{:S(2)}, u32[]{:S(2)}) async-start(bf16[16,8,2048]{2,1,0:T(8,128)(2,1)} %shard_map.82), calls=%async_computation | async-start | bytes 1048576 | tf_op jit(solution)/shard_map/all_to_all | solution.py:181
  18.0 1.1 %copy-start = (bf16[1024,400]{0,1:T(8,128)(2,1)S(1)}, bf16[1024,400]{0,1:T(8,128)(2,1)}, u32[]{:S(2)}) copy-start(bf16[1024,400]{0,1:T(8,128)(2,1)} %param.8) | copy-start | bytes 2457604
  19.1 0.7 %copy-start.2 = (s32[1024]{0:T(1024)S(1)}, s32[1024]{0:T(1024)}, u32[]{:S(2)}) copy-start(s32[1024]{0:T(1024)} %owner_slot_ref.1) | copy-start | bytes 12292
  19.8 0.7 copy-start.3
  31.1 6.8 %copy-start.1 = (bf16[8,128,128]{2,1,0:T(8,128)(2,1)S(1)}, bf16[8,128,128]{2,1,0:T(8,128)(2,1)}, u32[]{:S(2)}) copy-start(bf16[8,128,128]{2,1,0:T(8,128)(2,1)} %stiffness_ref.1) | copy-start | bytes 786436
  31.1 6.8 %copy-start.4 = (s32[8]{0:T(128)S(1)}, s32[8]{0:T(128)}, u32[]{:S(2)}) copy-start(s32[8]{0:T(128)} %partner_ref.1) | copy-start | bytes 100
  31.1 6.8 %collective-permute-start = (bf16[128,2048]{1,0:T(8,128)(2,1)S(1)}, bf16[128,2048]{1,0:T(8,128)(2,1)S(1)}, u32[]{:S(2)}, u32[]{:S(2)}) collective-permute-start(bf16[128,2048]{1,0:T(8,128)(2,1)S(1)} %bitcast.4), channel_id=1, source_target_pairs={{0,1},{1,0},{2,3},{3,2},{4,5},{5,4},{6,7},{7,6},{8,9},{9,8},{10,11... | collective-permute-start | bytes 1572872 | tf_op jit(solution)/shard_map/ppermute | solution.py:197

commit v6 on v5

--- a/solution.py
+++ b/solution.py
@@ -10,10 +10,11 @@
 SIZE = dict(zip(AXES, SIZES))
 SLOT_STEP = {"zlo": 256, "x": 64, "y": 8, "zhi": 4, "core": 2}
 FIRST = ("x", "core")
-SECOND = ("zlo", "y", "zhi")
+SECOND = ("y", "zhi", "zlo")
 N_FIRST = 8
 N_SECOND = 64
 N_ROW = 32
+GATHER_ORDER = [8 * zhi + 4 * y2 + 2 * y1 + y0 for zhi in (0, 1) for y1 in (0, 1) for y2 in (0, 1) for y0 in (0, 1)]
 NT = (((1,), (1,)), ((), ()))
 TN = (((0,), (0,)), ((), ()))
 VMEM = pl.BlockSpec(memory_space=pltpu.VMEM)
@@ -124,7 +125,8 @@
     target = lax.broadcasted_iota(jnp.int32, (modes, modes), 1)
     core = (source // half + lax.axis_index("core")) % 2
     peer = half // 8 - 1 - (source % half) // 8
-    ordered = peer % 8 * 32 + peer // 8 * 16 + core * 8 + source % 8
+    y = peer % 2 + peer // 4 % 2 * 2 + peer // 2 % 2 * 4
+    ordered = y * 32 + peer // 8 * 16 + core * 8 + source % 8
     move = (ordered == target).astype(jnp.float32).astype(jnp.bfloat16)
     energy = jnp.dot(energy, move, preferred_element_type=jnp.float32).astype(jnp.bfloat16)
     for i in range(out_ref.shape[0]):
@@ -176,8 +178,8 @@
     )(packet)
 
 
-def exchange(blocks, axes):
-    members = list(range(blocks.shape[0]))[::-1]
+def exchange(blocks, axes, order=None):
+    members = list(order or range(blocks.shape[0]))[::-1]
     return lax.all_to_all(blocks, axes, 0, 0, axis_index_groups=[members], tiled=True)
 
 
@@ -190,7 +192,7 @@
     width = nc + nf + -(nc + nf) % 128
 
     sent = packets(coord_con[0], coord_fixed[0], N_ROW // 2, width)
-    own = exchange(sent, ("zhi", "y")).reshape(modes // 2, width)
+    own = exchange(sent, ("zhi", "y"), GATHER_ORDER).reshape(modes // 2, width)
 
     phi, codes = early(elem_zone, owner_slot, phi_rows.T, width - nc)
     own, phi, codes = lax.optimization_barrier((own, phi, codes))

time: 66.8 us -> 66.7 us (level)
  starting transfers between devices: 21.3 us -> 20.5 us
    ppermute x1, starting transfers between devices: 4.86 us -> 4.1 us  [on_device(): other = lax.ppermute(own, 'core', [(0, 1), (1, 0)])]
where the time goes in v6:
time: 66.7 us; the launch traced here: 66.2 us
  blocking collectives  24.8 us (37%)
  starting transfers between devices  20.5 us (31%)
  waiting for transfers between devices  10.1 us (15%)
  Pallas kernels  7.59 us (11%)
  local copies, waits for them, and re-layouts  2.53 us (4%)
  other arithmetic  0.67 us (1%)
    all_to_all x2, blocking collectives, exchange(): lax.all_to_all(blocks, axes, 0, 0, axis_index_groups=[members], tiled=True)  24.8 us
    all_to_all x1, starting transfers between devices, exchange(): lax.all_to_all(blocks, axes, 0, 0, axis_index_groups=[members], tiled=True)  16.4 us
    all_to_all x1, waiting for transfers between devices, exchange(): lax.all_to_all(blocks, axes, 0, 0, axis_index_groups=[members], tiled=True)  10 us
    ppermute x1, starting transfers between devices, on_device(): other = lax.ppermute(own, 'core', [(0, 1), (1, 0)])  4.1 us
    pallas_call x1, Pallas kernels, block_energy(): pl.pallas_call(energy_kernel, out_shape=jax.ShapeDtypeStruct((copies, nbl...  2.86 us
    unnamed x10, local copies, waits for them, and re-layouts  2.49 us
    pallas_call x1, Pallas kernels, fetched(): pl.pallas_call(fetch_kernel, out_shape=pltpu.VMEM(psi.shape, psi.dtype),...  1.88 us
    pallas_call x1, Pallas kernels, packets(): pl.pallas_call(packet_kernel, out_shape=jax.ShapeDtypeStruct((copies, con...  1.59 us
  transfers between devices with their start and end apart: 2, of which 1 were waited for; matrix products, arithmetic and copies ran while one was open for 0% of the time, Pallas kernels for 4%

profile of v6, /device:TPU:1, one launch (start us, length us, event | category | flops | bytes accessed | tf_op | source)
XLA Modules:
  0.0 66.2 jit_solution(1234142700449879397)
XLA Ops:
  0.0 1.6 %shard_map.82 = bf16[16,8,2048]{2,1,0:T(8,128)(2,1)} custom-call(bf16[8,1536]{1,0:T(8,128)(2,1)} %bitcast.7, bf16[8,400]{1,0:T(8,128)(2,1)} %bitcast.8), custom_call_target="tpu_custom_call" | custom-call | tf_op jit(solution)/shard_map/pallas_call | solution.py:38
  1.6 16.4 %all-to-all-start = ((bf16[16,8,2048]{2,1,0:T(8,128)(2,1)}), bf16[16,8,2048]{2,1,0:T(8,128)(2,1)S(1)}, u32[]{:S(2)}, u32[]{:S(2)}) async-start(bf16[16,8,2048]{2,1,0:T(8,128)(2,1)} %shard_map.82), calls=%async_computation | async-start | bytes 1048576 | tf_op jit(solution)/shard_map/all_to_all | solution.py:183
  18.0 0.0 copy-start
  18.0 1.1 %copy-done = bf16[1024,400]{0,1:T(8,128)(2,1)S(1)} copy-done((bf16[1024,400]{0,1:T(8,128)(2,1)S(1)}, bf16[1024,400]{0,1:T(8,128)(2,1)}, u32[]{:S(2)}) %copy-start) | copy-done | bytes 819224
  19.1 0.0 copy-start.2
  19.1 0.7 %copy-done.2 = s32[1024]{0:T(1024)S(1)} copy-done((s32[1024]{0:T(1024)S(1)}, s32[1024]{0:T(1024)}, u32[]{:S(2)}) %copy-start.2) | copy-done | bytes 4120
  19.8 0.0 copy-start.3
  19.8 0.7 copy-done.3
  20.5 0.9 %shard_map.83 = (bf16[1024,512]{1,0:T(8,128)(2,1)S(1)}, bf16[8,128]{1,0:T(8,128)(2,1)S(1)}) custom-call(s32[8]{0:T(128)S(1)} %copy-done.3, s32[1024]{0:T(1024)S(1)} %copy-done.2, bf16[400,1024]{1,0:T(8,128)(2,1)S(1)} %bitcast.6), custom_call_target="tpu_custom_call" | custom-call | bytes 8388608 | tf_op jit(solution)/shard_map/pallas_call | solution.py:62
  21.4 10.0 %all-to-all-done = bf16[16,8,2048]{2,1,0:T(8,128)(2,1)S(1)} async-done(((bf16[16,8,2048]{2,1,0:T(8,128)(2,1)}), bf16[16,8,2048]{2,1,0:T(8,128)(2,1)S(1)}, u32[]{:S(2)}, u32[]{:S(2)}) %all-to-all-start) | async-done | bytes 524320 | tf_op jit(solution)/shard_map/all_to_all | solution.py:183
  31.5 0.0 copy-start.1
  31.5 0.0 copy-start.4
  31.5 4.1 %collective-permute-start = (bf16[128,2048]{1,0:T(8,128)(2,1)S(1)}, bf16[128,2048]{1,0:T(8,128)(2,1)S(1)}, u32[]{:S(2)}, u32[]{:S(2)}) collective-permute-start(bf16[128,2048]{1,0:T(8,128)(2,1)S(1)} %bitcast.4), channel_id=1, source_target_pairs={{0,1},{1,0},{2,3},{3,2},{4,5},{5,4},{6,7},{7,6},{8,9},{9,8},{10,11... | collective-permute-start | bytes 1572872 | tf_op jit(solution)/shard_map/ppermute | solution.py:199
  35.6 1.9 %shard_map.84.psi_ref = bf16[1024,1536]{1,0:T(8,128)(2,1)S(1)} custom-call(bf16[1024,1536]{1,0:T(8,128)(2,1)} %psi_ref.1), custom_call_target="tpu_custom_call" | custom-call | bytes 6291456 | tf_op jit(solution)/shard_map/pallas_call | solution.py:90
  37.5 0.0 collective-permute-done.other_ref
  37.5 0.0 copy-done.1
  37.5 0.0 copy-done.4
  37.5 2.9 %shard_map.85 = bf16[8,8,384]{2,1,0:T(8,128)(2,1)S(1)} custom-call(s32[8]{0:T(128)S(1)} %copy-done.4, bf16[128,2048]{1,0:T(8,128)(2,1)S(1)} %bitcast.5, bf16[128,2048]{1,0:T(8,128)(2,1)S(1)} %collective-permute-done.other_ref, bf16[1024,512]{1,0:T(8,128)(2,1)S(1)} %get-tuple-element.13.phi_ref, bf16[1024,1536]{1,0:T(8,128)(2,1)S(1)} %shard_map.84.psi_ref, ...), custom_call_target="tpu_custom_call" | custom-call | flops 1073741824 | bytes 6291456 | tf_op jit(solution)/shard_map/pallas_call | solution.py:140
  40.4 7.8 %all_to_all.15.packet_ref = bf16[8,8,384]{2,1,0:T(8,128)(2,1)S(1)} all-to-all(bf16[8,8,384]{2,1,0:T(8,128)(2,1)S(1)} %shard_map.85), channel_id=1, replica_groups={{97,96,65,64,33,32,1,0},{99,98,67,66,35,34,3,2},{101,100,69,68,37,36,5,..., dimensions={0} | all-to-all | bytes 98304 | tf_op jit(solution)/shard_map/all_to_all | solution.py:183
  48.2 0.3 shard_map.86
  48.6 17.0 %all_to_all.16 = bf16[64,2,256]{2,1,0:T(2,128)(2,1)S(1)} all-to-all(bf16[64,2,256]{2,1,0:T(2,128)(2,1)S(1)} %reshape.7), channel_id=1, replica_groups={{414,286,158,30,412,284,156,28,410,282,154,26,408,280,152,24,406,278,15..., dimensions={0} | all-to-all | bytes 131072 | tf_op jit(solution)/shard_map/all_to_all | solution.py:183
  65.6 0.7 %convert_reduce_fusion = f32[2,256]{1,0:T(2,128)} fusion(bf16[64,2,256]{2,1,0:T(2,128)(2,1)S(1)} %all_to_all.16), kind=kLoop, calls=%fused_computation | loop fusion | flops 65024 | bytes 67584 | tf_op jit(solution)/shard_map/reduce_sum | solution.py:206
  (1 shorter events, 0.0 us)
Async XLA Ops:
  1.6 29.9 %all-to-all-start = ((bf16[16,8,2048]{2,1,0:T(8,128)(2,1)}), bf16[16,8,2048]{2,1,0:T(8,128)(2,1)S(1)}, u32[]{:S(2)}, u32[]{:S(2)}) async-start(bf16[16,8,2048]{2,1,0:T(8,128)(2,1)} %shard_map.82), calls=%async_computation | async-start | bytes 1048576 | tf_op jit(solution)/shard_map/all_to_all | solution.py:183
  18.0 1.1 %copy-start = (bf16[1024,400]{0,1:T(8,128)(2,1)S(1)}, bf16[1024,400]{0,1:T(8,128)(2,1)}, u32[]{:S(2)}) copy-start(bf16[1024,400]{0,1:T(8,128)(2,1)} %param.8) | copy-start | bytes 2457604
  19.1 0.7 %copy-start.2 = (s32[1024]{0:T(1024)S(1)}, s32[1024]{0:T(1024)}, u32[]{:S(2)}) copy-start(s32[1024]{0:T(1024)} %owner_slot_ref.1) | copy-start | bytes 12292
  19.8 0.7 copy-start.3
  31.5 6.0 %copy-start.1 = (bf16[8,128,128]{2,1,0:T(8,128)(2,1)S(1)}, bf16[8,128,128]{2,1,0:T(8,128)(2,1)}, u32[]{:S(2)}) copy-start(bf16[8,128,128]{2,1,0:T(8,128)(2,1)} %stiffness_ref.1) | copy-start | bytes 786436
  31.5 6.0 %copy-start.4 = (s32[8]{0:T(128)S(1)}, s32[8]{0:T(128)}, u32[]{:S(2)}) copy-start(s32[8]{0:T(128)} %partner_ref.1) | copy-start | bytes 100
  31.5 6.0 %collective-permute-start = (bf16[128,2048]{1,0:T(8,128)(2,1)S(1)}, bf16[128,2048]{1,0:T(8,128)(2,1)S(1)}, u32[]{:S(2)}, u32[]{:S(2)}) collective-permute-start(bf16[128,2048]{1,0:T(8,128)(2,1)S(1)} %bitcast.4), channel_id=1, source_target_pairs={{0,1},{1,0},{2,3},{3,2},{4,5},{5,4},{6,7},{7,6},{8,9},{9,8},{10,11... | collective-permute-start | bytes 1572872 | tf_op jit(solution)/shard_map/ppermute | solution.py:199

commit v7 on v5

--- a/solution.py
+++ b/solution.py
@@ -43,7 +43,7 @@
     )(con, fixed)
 
 
-def early_kernel(elem_zone_ref, owner_slot_ref, phi_ref, rows_ref, codes_ref):
+def early_kernel(elem_zone_ref, owner_slot_ref, phi_ref, rows_ref, codes_ref, move_ref):
     nf, rows = phi_ref.shape
     rows_ref[:, :nf] = phi_ref[...].T
     rows_ref[:, nf:] = jnp.zeros((rows, rows_ref.shape[1] - nf), rows_ref.dtype)
@@ -55,17 +55,27 @@
         codes = jnp.where((row == b) & (lane == 0), slot // 32, codes)
         codes = jnp.where((row == b) & (lane == 1), slot % 32, codes)
     codes_ref[...] = codes.astype(jnp.float32).astype(codes_ref.dtype)
-
-
-def early(elem_zone, owner_slot, phi_t, width):
+    modes = move_ref.shape[0]
+    half = modes // 2
+    source = lax.broadcasted_iota(jnp.int32, (modes, modes), 0)
+    target = lax.broadcasted_iota(jnp.int32, (modes, modes), 1)
+    core = (source // half + lax.axis_index("core")) % 2
+    peer = half // 8 - 1 - (source % half) // 8
+    ordered = peer % 8 * 32 + peer // 8 * 16 + core * 8 + source % 8
+    move = (ordered == target).astype(jnp.float32).astype(jnp.bfloat16)
+    move_ref[...] = move
+
+
+def early(elem_zone, owner_slot, phi_t, width, modes):
     return pl.pallas_call(
         early_kernel,
         out_shape=(
             jax.ShapeDtypeStruct((phi_t.shape[1], width), phi_t.dtype),
             jax.ShapeDtypeStruct((elem_zone.shape[0], CODE_LANES), jnp.bfloat16),
+            jax.ShapeDtypeStruct((modes, modes), jnp.bfloat16),
         ),
         in_specs=[SMEM, SMEM, VMEM],
-        out_specs=(VMEM, VMEM),
+        out_specs=(VMEM, VMEM, VMEM),
         compiler_params=pltpu.CompilerParams(vmem_limit_bytes=16 * 2**20),
         cost_estimate=pl.CostEstimate(flops=0, bytes_accessed=8 * 2**20, transcendentals=0),
     )(elem_zone, owner_slot, phi_t)
@@ -98,7 +108,7 @@
 
 
 def energy_kernel(
-    partner_ref, own_ref, other_ref, phi_ref, psi_ref, stiffness_ref, codes_ref, out_ref, coords, shapes
+    partner_ref, own_ref, other_ref, phi_ref, psi_ref, stiffness_ref, codes_ref, move_ref, out_ref, coords, shapes
 ):
     half = other_ref.shape[0]
     nc = psi_ref.shape[1]
@@ -120,25 +130,19 @@
         pushed = jnp.dot(stiffness_ref[b], relative, preferred_element_type=jnp.float32)
         sums.append(jnp.sum(relative.astype(jnp.float32) * pushed, axis=0, keepdims=True))
     energy = jnp.concatenate(sums, axis=0).astype(jnp.bfloat16)
-    source = lax.broadcasted_iota(jnp.int32, (modes, modes), 0)
-    target = lax.broadcasted_iota(jnp.int32, (modes, modes), 1)
-    core = (source // half + lax.axis_index("core")) % 2
-    peer = half // 8 - 1 - (source % half) // 8
-    ordered = peer % 8 * 32 + peer // 8 * 16 + core * 8 + source % 8
-    move = (ordered == target).astype(jnp.float32).astype(jnp.bfloat16)
-    energy = jnp.dot(energy, move, preferred_element_type=jnp.float32).astype(jnp.bfloat16)
+    energy = jnp.dot(energy, move_ref[...], preferred_element_type=jnp.float32).astype(jnp.bfloat16)
     for i in range(out_ref.shape[0]):
         out_ref[i, :, :modes] = energy
         out_ref[i, :, modes:] = codes_ref[...]
 
 
-def block_energy(partner, own, other, phi, psi, stiffness, codes, copies):
+def block_energy(partner, own, other, phi, psi, stiffness, codes, move, copies):
     nblocks, block, _ = stiffness.shape
     modes = 2 * other.shape[0]
     return pl.pallas_call(
         energy_kernel,
         out_shape=jax.ShapeDtypeStruct((copies, nblocks, modes + CODE_LANES), jnp.bfloat16),
-        in_specs=[SMEM, VMEM, VMEM, VMEM, VMEM, VMEM, VMEM],
+        in_specs=[SMEM, VMEM, VMEM, VMEM, VMEM, VMEM, VMEM, VMEM],
         out_specs=VMEM,
         scratch_shapes=[
             pltpu.VMEM((modes, own.shape[1]), jnp.bfloat16),
@@ -146,7 +150,7 @@
         ],
         compiler_params=pltpu.CompilerParams(vmem_limit_bytes=24 * 2**20),
         cost_estimate=pl.CostEstimate(flops=2**30, bytes_accessed=6 * 2**20, transcendentals=0),
-    )(partner, own, other, phi, psi, stiffness, codes)
+    )(partner, own, other, phi, psi, stiffness, codes, move)
 
 
 def zone_kernel(packet_ref, out_ref):
@@ -192,12 +196,12 @@
     sent = packets(coord_con[0], coord_fixed[0], N_ROW // 2, width)
     own = exchange(sent, ("zhi", "y")).reshape(modes // 2, width)
 
-    phi, codes = early(elem_zone, owner_slot, phi_rows.T, width - nc)
-    own, phi, codes = lax.optimization_barrier((own, phi, codes))
+    phi, codes, move = early(elem_zone, owner_slot, phi_rows.T, width - nc, modes)
+    own, phi, codes, move = lax.optimization_barrier((own, phi, codes, move))
     other = lax.ppermute(own, "core", [(0, 1), (1, 0)])
 
     psi = fetched(psi_rows)
-    energy = block_energy(partner, own, other, phi, psi, stiffness, codes, N_FIRST)
+    energy = block_energy(partner, own, other, phi, psi, stiffness, codes, move, N_FIRST)
     gathered = exchange(energy, FIRST)
     partial_sums = zone_sums(gathered, 2 * N_SECOND).reshape(N_SECOND, 2, modes)
     received = exchange(partial_sums, SECOND)

time: 66.8 us -> 66.7 us (level)
  transfers between devices with their start and end apart: 2 -> 2, of which waited for: 1 -> 1; matrix products, arithmetic and copies ran while one was open for 0% -> 0% of each run, Pallas kernels for 4% -> 5%
where the time goes in v7:
time: 66.7 us; the launch traced here: 66 us
  blocking collectives  24.6 us (37%)
  starting transfers between devices  21.3 us (32%)
  waiting for transfers between devices  9.48 us (14%)
  Pallas kernels  7.48 us (11%)
  local copies, waits for them, and re-layouts  2.53 us (4%)
  other arithmetic  0.67 us (1%)
    all_to_all x2, blocking collectives, exchange(): lax.all_to_all(blocks, axes, 0, 0, axis_index_groups=[members], tiled=True)  24.6 us
    all_to_all x1, starting transfers between devices, exchange(): lax.all_to_all(blocks, axes, 0, 0, axis_index_groups=[members], tiled=True)  16.4 us
    all_to_all x1, waiting for transfers between devices, exchange(): lax.all_to_all(blocks, axes, 0, 0, axis_index_groups=[members], tiled=True)  9.48 us
    ppermute x1, starting transfers between devices, on_device(): other = lax.ppermute(own, 'core', [(0, 1), (1, 0)])  4.86 us
    pallas_call x1, Pallas kernels, block_energy(): pl.pallas_call(energy_kernel, out_shape=jax.ShapeDtypeStruct((copies, nbl...  2.5 us
    unnamed x10, local copies, waits for them, and re-layouts  2.49 us
    pallas_call x1, Pallas kernels, fetched(): pl.pallas_call(fetch_kernel, out_shape=pltpu.VMEM(psi.shape, psi.dtype),...  1.88 us
    pallas_call x1, Pallas kernels, packets(): pl.pallas_call(packet_kernel, out_shape=jax.ShapeDtypeStruct((copies, con...  1.59 us
  transfers between devices with their start and end apart: 2, of which 1 were waited for; matrix products, arithmetic and copies ran while one was open for 0% of the time, Pallas kernels for 5%

profile of v7, /device:TPU:1, one launch (start us, length us, event | category | flops | bytes accessed | tf_op | source)
XLA Modules:
  0.0 66.0 jit_solution(4207486891055384418)
XLA Ops:
  0.0 1.6 %shard_map.82 = bf16[16,8,2048]{2,1,0:T(8,128)(2,1)} custom-call(bf16[8,1536]{1,0:T(8,128)(2,1)} %bitcast.7, bf16[8,400]{1,0:T(8,128)(2,1)} %bitcast.8), custom_call_target="tpu_custom_call" | custom-call | tf_op jit(solution)/shard_map/pallas_call | solution.py:37
  1.6 16.4 %all-to-all-start = ((bf16[16,8,2048]{2,1,0:T(8,128)(2,1)}), bf16[16,8,2048]{2,1,0:T(8,128)(2,1)S(1)}, u32[]{:S(2)}, u32[]{:S(2)}) async-start(bf16[16,8,2048]{2,1,0:T(8,128)(2,1)} %shard_map.82), calls=%async_computation | async-start | bytes 1048576 | tf_op jit(solution)/shard_map/all_to_all | solution.py:185
  18.0 0.0 copy-start
  18.0 1.1 %copy-done = bf16[1024,400]{0,1:T(8,128)(2,1)S(1)} copy-done((bf16[1024,400]{0,1:T(8,128)(2,1)S(1)}, bf16[1024,400]{0,1:T(8,128)(2,1)}, u32[]{:S(2)}) %copy-start) | copy-done | bytes 819224
  19.1 0.0 copy-start.2
  19.1 0.7 %copy-done.2 = s32[1024]{0:T(1024)S(1)} copy-done((s32[1024]{0:T(1024)S(1)}, s32[1024]{0:T(1024)}, u32[]{:S(2)}) %copy-start.2) | copy-done | bytes 4120
  19.8 0.0 copy-start.4
  19.8 0.7 copy-done.4
  20.5 1.2 %shard_map.83 = (bf16[1024,512]{1,0:T(8,128)(2,1)S(1)}, bf16[8,128]{1,0:T(8,128)(2,1)S(1)}, bf16[256,256]{1,0:T(8,128)(2,1)S(1)}) custom-call(s32[8]{0:T(128)S(1)} %copy-done.4, s32[1024]{0:T(1024)S(1)} %copy-done.2, bf16[400,1024]{1,0:T(8,128)(2,1)S(1)} %bitcast.6), custom_call_target="tpu_custom_call" | custom-call | bytes 8388608 | tf_op jit(solution)/shard_map/pallas_call | solution.py:70
  21.7 9.5 %all-to-all-done = bf16[16,8,2048]{2,1,0:T(8,128)(2,1)S(1)} async-done(((bf16[16,8,2048]{2,1,0:T(8,128)(2,1)}), bf16[16,8,2048]{2,1,0:T(8,128)(2,1)S(1)}, u32[]{:S(2)}, u32[]{:S(2)}) %all-to-all-start) | async-done | bytes 524320 | tf_op jit(solution)/shard_map/all_to_all | solution.py:185
  31.1 0.0 copy-start.1
  31.1 0.0 copy-start.3
  31.1 4.9 %collective-permute-start = (bf16[128,2048]{1,0:T(8,128)(2,1)S(1)}, bf16[128,2048]{1,0:T(8,128)(2,1)S(1)}, u32[]{:S(2)}, u32[]{:S(2)}) collective-permute-start(bf16[128,2048]{1,0:T(8,128)(2,1)S(1)} %bitcast.4), channel_id=1, source_target_pairs={{0,1},{1,0},{2,3},{3,2},{4,5},{5,4},{6,7},{7,6},{8,9},{9,8},{10,11... | collective-permute-start | bytes 1572872 | tf_op jit(solution)/shard_map/ppermute | solution.py:201
  36.0 1.9 %shard_map.84.psi_ref = bf16[1024,1536]{1,0:T(8,128)(2,1)S(1)} custom-call(bf16[1024,1536]{1,0:T(8,128)(2,1)} %psi_ref.1), custom_call_target="tpu_custom_call" | custom-call | bytes 6291456 | tf_op jit(solution)/shard_map/pallas_call | solution.py:99
  37.9 0.0 collective-permute-done.other_ref
  37.9 0.0 copy-done.1
  37.9 0.0 copy-done.3
  37.9 2.5 %shard_map.85 = bf16[8,8,384]{2,1,0:T(8,128)(2,1)S(1)} custom-call(s32[8]{0:T(128)S(1)} %copy-done.3, bf16[128,2048]{1,0:T(8,128)(2,1)S(1)} %bitcast.5, bf16[128,2048]{1,0:T(8,128)(2,1)S(1)} %collective-permute-done.other_ref, bf16[1024,512]{1,0:T(8,128)(2,1)S(1)} %get-tuple-element.16.phi_ref, bf16[1024,1536]{1,0:T(8,128)(2,1)S(1)} %shard_map.84.psi_ref, ...), custom_call_target="tpu_custom_call" | custom-call | flops 1073741824 | bytes 6291456 | tf_op jit(solution)/shard_map/pallas_call | solution.py:142
  40.4 7.9 %all_to_all.15.packet_ref = bf16[8,8,384]{2,1,0:T(8,128)(2,1)S(1)} all-to-all(bf16[8,8,384]{2,1,0:T(8,128)(2,1)S(1)} %shard_map.85), channel_id=1, replica_groups={{97,96,65,64,33,32,1,0},{99,98,67,66,35,34,3,2},{101,100,69,68,37,36,5,..., dimensions={0} | all-to-all | bytes 98304 | tf_op jit(solution)/shard_map/all_to_all | solution.py:185
  48.3 0.3 shard_map.86
  48.7 16.7 %all_to_all.16 = bf16[64,2,256]{2,1,0:T(2,128)(2,1)S(1)} all-to-all(bf16[64,2,256]{2,1,0:T(2,128)(2,1)S(1)} %reshape.7), channel_id=1, replica_groups={{414,412,410,408,406,404,402,400,398,396,394,392,390,388,386,384,286,28..., dimensions={0} | all-to-all | bytes 131072 | tf_op jit(solution)/shard_map/all_to_all | solution.py:185
  65.4 0.7 %convert_reduce_fusion = f32[2,256]{1,0:T(2,128)} fusion(bf16[64,2,256]{2,1,0:T(2,128)(2,1)S(1)} %all_to_all.16), kind=kLoop, calls=%fused_computation | loop fusion | flops 65024 | bytes 67584 | tf_op jit(solution)/shard_map/reduce_sum | solution.py:208
  (1 shorter events, 0.0 us)
Async XLA Ops:
  1.6 29.5 %all-to-all-start = ((bf16[16,8,2048]{2,1,0:T(8,128)(2,1)}), bf16[16,8,2048]{2,1,0:T(8,128)(2,1)S(1)}, u32[]{:S(2)}, u32[]{:S(2)}) async-start(bf16[16,8,2048]{2,1,0:T(8,128)(2,1)} %shard_map.82), calls=%async_computation | async-start | bytes 1048576 | tf_op jit(solution)/shard_map/all_to_all | solution.py:185
  18.0 1.1 %copy-start = (bf16[1024,400]{0,1:T(8,128)(2,1)S(1)}, bf16[1024,400]{0,1:T(8,128)(2,1)}, u32[]{:S(2)}) copy-start(bf16[1024,400]{0,1:T(8,128)(2,1)} %param.8) | copy-start | bytes 2457604
  19.1 0.7 %copy-start.2 = (s32[1024]{0:T(1024)S(1)}, s32[1024]{0:T(1024)}, u32[]{:S(2)}) copy-start(s32[1024]{0:T(1024)} %owner_slot_ref.1) | copy-start | bytes 12292
  19.8 0.7 copy-start.4
  31.1 6.8 %copy-start.1 = (bf16[8,128,128]{2,1,0:T(8,128)(2,1)S(1)}, bf16[8,128,128]{2,1,0:T(8,128)(2,1)}, u32[]{:S(2)}) copy-start(bf16[8,128,128]{2,1,0:T(8,128)(2,1)} %stiffness_ref.1) | copy-start | bytes 786436
  31.1 6.8 %copy-start.3 = (s32[8]{0:T(128)S(1)}, s32[8]{0:T(128)}, u32[]{:S(2)}) copy-start(s32[8]{0:T(128)} %partner_ref.1) | copy-start | bytes 100
  31.1 6.8 %collective-permute-start = (bf16[128,2048]{1,0:T(8,128)(2,1)S(1)}, bf16[128,2048]{1,0:T(8,128)(2,1)S(1)}, u32[]{:S(2)}, u32[]{:S(2)}) collective-permute-start(bf16[128,2048]{1,0:T(8,128)(2,1)S(1)} %bitcast.4), channel_id=1, source_target_pairs={{0,1},{1,0},{2,3},{3,2},{4,5},{5,4},{6,7},{7,6},{8,9},{9,8},{10,11... | collective-permute-start | bytes 1572872 | tf_op jit(solution)/shard_map/ppermute | solution.py:201
